TPU v7x, 32 devices: a whole 2x2x4 slice. The times are simulated.
32 devices in a mesh: seq: 8 (over y, x, core), tensor: 4 (over z).
Axes of the slice: x: 2, y: 2, z: 4, core: 2. Of those that a mesh axis runs over, the one named last changes fastest.
Arguments:
- inputs: float32 [8192, 2048], P('seq', 'tensor'), may hold values from -6 to 6
- cotangent: float32 [8192, 2048], P('seq', 'tensor'), may hold values from -6 to 6
- proj_in: bfloat16 [2048, 6, 2048], P('seq', None, 'tensor'), may hold values from -0.125 to 0.125
- proj_out: bfloat16 [2048, 2, 2048], P('seq', None, 'tensor'), may hold values from -4 to 4
- ffn_in: bfloat16 [2048, 4, 5504], P('seq', None, 'tensor'), may hold values from -0.125 to 0.125
- ffn_down: bfloat16 [2048, 2, 5504], P('seq', None, 'tensor'), may hold values from -0.078125 to 0.078125
- gains: bfloat16 [2048, 5], P('seq'), may hold values from 0.5 to 1.5
Outputs:
- output: float32 [8192, 2048], P('seq', 'tensor')
- grad_inputs: float32 [8192, 2048], P('seq', 'tensor')
- grad_proj_in: float32 [2048, 6, 2048], P('seq', None, 'tensor')
- grad_proj_out: float32 [2048, 2, 2048], P('seq', None, 'tensor')
- grad_ffn_in: float32 [2048, 4, 5504], P('seq', None, 'tensor')
- grad_ffn_down: float32 [2048, 2, 5504], P('seq', None, 'tensor')
- grad_gains: float32 [2048, 5], P('seq')
All inputs are finite; a program needn't handle non-finite values.
Results may differ from a plain program's by a relative error of at most 0.035.
Values may be sent and summed in bfloat16 or wider, within the bound.
A program may use at most 384 MiB of HBM per device.

v0:
```python
import jax
import jax.numpy as jnp
from jax import lax
from jax.sharding import PartitionSpec as P

HEAD_DIM = 128
WINDOW = 1024


epsilon = 1e-06
floor_score = -1e30


def shifted(block, axis, distance):
    devices = range(lax.axis_size(axis))
    route = [(i - distance, i) for i in devices if i - distance in devices]
    return lax.ppermute(block, axis, route)


def widen(shard_rows):
    return lax.all_gather(shard_rows.astype(jnp.bfloat16), "tensor", axis=1, tiled=True).astype(
        shard_rows.dtype
    )


def widen_grad(shard_rows):
    return lax.all_gather(shard_rows.astype(jnp.bfloat16), "tensor", axis=1, tiled=True)


def narrow(partial_value):
    return lax.psum_scatter(
        partial_value.astype(jnp.bfloat16), "tensor", scatter_dimension=1, tiled=True
    ).astype(jnp.float32)


def normalize(full_rows, gain_col):
    inverse = lax.rsqrt(jnp.mean(full_rows * full_rows, axis=1, keepdims=True) + epsilon)
    return (inverse, (full_rows * inverse * gain_col.astype(jnp.float32)).astype(jnp.bfloat16))


def norm_back(full_rows, inverse, gain_col, gradient):
    scaled = gradient * gain_col.astype(jnp.float32)
    cubed = inverse * inverse * inverse
    dfull = inverse * scaled - full_rows * cubed * jnp.mean(
        scaled * full_rows, axis=1, keepdims=True
    )
    return (dfull, jnp.sum(gradient * full_rows * inverse, axis=0))


def allowed(query_pos, key_pos, horizon):
    later = key_pos[None, :] <= query_pos[:, None]
    nearby = key_pos[None, :] > query_pos[:, None] - horizon
    return (later & nearby & (key_pos[None, :] >= 0))[None]


def split_heads(rows, length):
    return rows.reshape(length, rows.shape[1] // HEAD_DIM, HEAD_DIM)


def block_scores(query_rows, key_rows, query_pos, key_pos, horizon):
    scores = jnp.einsum(
        "rhe,khe->hrk", query_rows, key_rows, preferred_element_type=jnp.float32
    ) * HEAD_DIM ** (-0.5)
    allowed_mask = allowed(query_pos, key_pos, horizon)
    return (jnp.where(allowed_mask, scores, floor_score), allowed_mask)


def attention_forward(queries, pairs, query_pos, key_pos, horizon, spans):
    results, saved_stats = ([], [])
    for offset, length, anchor, extent in spans:
        query_rows = split_heads(queries[offset : offset + length], length)
        key_rows = split_heads(pairs[anchor : anchor + extent, 0], extent)
        value_rows = split_heads(pairs[anchor : anchor + extent, 1], extent)
        masked, allowed_mask = block_scores(
            query_rows,
            key_rows,
            query_pos[offset : offset + length],
            key_pos[anchor : anchor + extent],
            horizon,
        )
        highest_score = jnp.max(masked, axis=2, keepdims=True)
        exponent = jnp.where(allowed_mask, jnp.exp(masked - highest_score), 0.0)
        summed = jnp.sum(exponent, axis=2, keepdims=True)
        probability = (exponent / summed).astype(jnp.bfloat16)
        result = jnp.einsum(
            "hrk,khe->rhe", probability, value_rows, preferred_element_type=jnp.float32
        )
        results.append(result.reshape(length, -1))
        saved_stats.append((highest_score, summed))
    return (jnp.concatenate(results, axis=0).astype(jnp.bfloat16), saved_stats)


def attention_backward(queries, pairs, query_pos, key_pos, horizon, spans, saved_stats, dresult):
    dquery_parts = []
    dpairs = jnp.zeros(pairs.shape, jnp.float32)
    for (offset, length, anchor, extent), (highest_score, summed) in zip(spans, saved_stats):
        query_rows = split_heads(queries[offset : offset + length], length)
        key_rows = split_heads(pairs[anchor : anchor + extent, 0], extent)
        value_rows = split_heads(pairs[anchor : anchor + extent, 1], extent)
        dout_rows = split_heads(dresult[offset : offset + length], length)
        masked, allowed_mask = block_scores(
            query_rows,
            key_rows,
            query_pos[offset : offset + length],
            key_pos[anchor : anchor + extent],
            horizon,
        )
        probability = jnp.where(allowed_mask, jnp.exp(masked - highest_score), 0.0) / summed
        dvalues = jnp.einsum(
            "hrk,rhe->khe",
            probability.astype(jnp.bfloat16),
            dout_rows,
            preferred_element_type=jnp.float32,
        )
        dprobability = jnp.einsum(
            "rhe,khe->hrk", dout_rows, value_rows, preferred_element_type=jnp.float32
        )
        row_dot = jnp.sum(probability * dprobability, axis=2, keepdims=True)
        dscores = (probability * (dprobability - row_dot)).astype(jnp.bfloat16)
        dqueries = jnp.einsum(
            "hrk,khe->rhe", dscores, key_rows, preferred_element_type=jnp.float32
        ) * HEAD_DIM ** (-0.5)
        dkeys = jnp.einsum(
            "hrk,rhe->khe", dscores, query_rows, preferred_element_type=jnp.float32
        ) * HEAD_DIM ** (-0.5)
        dquery_parts.append(dqueries.reshape(length, -1))
        stacked = jnp.stack([dkeys.reshape(extent, -1), dvalues.reshape(extent, -1)], axis=1)
        dpairs = dpairs.at[anchor : anchor + extent].add(stacked)
    return (jnp.concatenate(dquery_parts, axis=0).astype(jnp.bfloat16), dpairs)


def far_block(query_rows, cache_kv, query_pos, start, extent, horizon):
    pieces = lax.dynamic_slice_in_dim(cache_kv, start, extent, 0)
    key_rows = split_heads(pieces[:, 0], extent)
    value_rows = split_heads(pieces[:, 1], extent)
    key_pos = start + jnp.arange(extent, dtype=jnp.int32)
    masked, allowed_mask = block_scores(query_rows, key_rows, query_pos, key_pos, horizon)
    return (masked, allowed_mask, key_rows, value_rows)


def far_forward(queries, cache_kv, query_pos, extent):
    horizon = cache_kv.shape[0] + 1
    results, saved_stats = ([], [])
    for offset in range(0, queries.shape[0], extent):
        query_rows = split_heads(queries[offset : offset + extent], extent)
        block_pos = query_pos[offset : offset + extent]
        count = block_pos[extent - 1] // extent + 1
        heads = query_rows.shape[1]

        def stat_step(index, carry):
            top, summed = carry
            masked, allowed_mask, key_rows, value_rows = far_block(
                query_rows, cache_kv, block_pos, index * extent, extent, horizon
            )
            new_top = jnp.maximum(top, jnp.max(masked, axis=2, keepdims=True))
            fresh = jnp.sum(
                jnp.where(allowed_mask, jnp.exp(masked - new_top), 0.0), axis=2, keepdims=True
            )
            return (new_top, summed * jnp.exp(top - new_top) + fresh)

        start_stats = (
            jnp.full((heads, extent, 1), floor_score, jnp.float32),
            jnp.zeros((heads, extent, 1), jnp.float32),
        )
        top, summed = lax.fori_loop(0, count, stat_step, start_stats)

        def value_step(index, total):
            masked, allowed_mask, key_rows, value_rows = far_block(
                query_rows, cache_kv, block_pos, index * extent, extent, horizon
            )
            probability = (jnp.where(allowed_mask, jnp.exp(masked - top), 0.0) / summed).astype(
                jnp.bfloat16
            )
            return total + jnp.einsum(
                "hrk,khe->rhe", probability, value_rows, preferred_element_type=jnp.float32
            )

        result = lax.fori_loop(
            0, count, value_step, jnp.zeros((extent, heads, HEAD_DIM), jnp.float32)
        )
        results.append(result.reshape(extent, -1))
        saved_stats.append((top, summed))
    return (jnp.concatenate(results, axis=0).astype(jnp.bfloat16), saved_stats)


def far_backward(queries, cache_kv, query_pos, extent, saved_stats, dresult):
    horizon = cache_kv.shape[0] + 1
    dquery_parts = []
    dcache_all = jnp.zeros(cache_kv.shape, jnp.float32)
    for block_number, (top, summed) in enumerate(saved_stats):
        offset = block_number * extent
        query_rows = split_heads(queries[offset : offset + extent], extent)
        dout_rows = split_heads(dresult[offset : offset + extent], extent)
        block_pos = query_pos[offset : offset + extent]
        count = block_pos[extent - 1] // extent + 1
        heads = query_rows.shape[1]

        def weights_of(index):
            masked, allowed_mask, key_rows, value_rows = far_block(
                query_rows, cache_kv, block_pos, index * extent, extent, horizon
            )
            probability = jnp.where(allowed_mask, jnp.exp(masked - top), 0.0) / summed
            dprobability = jnp.einsum(
                "rhe,khe->hrk", dout_rows, value_rows, preferred_element_type=jnp.float32
            )
            return (probability, dprobability, key_rows)

        def dot_step(index, total):
            probability, dprobability, key_rows = weights_of(index)
            return total + jnp.sum(probability * dprobability, axis=2, keepdims=True)

        row_dot = lax.fori_loop(0, count, dot_step, jnp.zeros((heads, extent, 1), jnp.float32))

        def grad_step(index, carry):
            dquery_total, dcache_now = carry
            probability, dprobability, key_rows = weights_of(index)
            dvalues = jnp.einsum(
                "hrk,rhe->khe",
                probability.astype(jnp.bfloat16),
                dout_rows,
                preferred_element_type=jnp.float32,
            )
            dscores = (probability * (dprobability - row_dot)).astype(jnp.bfloat16)
            dquery_total = dquery_total + jnp.einsum(
                "hrk,khe->rhe", dscores, key_rows, preferred_element_type=jnp.float32
            ) * HEAD_DIM ** (-0.5)
            dkeys = jnp.einsum(
                "hrk,rhe->khe", dscores, query_rows, preferred_element_type=jnp.float32
            ) * HEAD_DIM ** (-0.5)
            stacked = jnp.stack([dkeys.reshape(extent, -1), dvalues.reshape(extent, -1)], axis=1)
            start = index * extent
            before = lax.dynamic_slice_in_dim(dcache_now, start, extent, 0)
            return (
                dquery_total,
                lax.dynamic_update_slice_in_dim(dcache_now, before + stacked, start, 0),
            )

        dquery_block, dcache_all = lax.fori_loop(
            0, count, grad_step, (jnp.zeros((extent, heads, HEAD_DIM), jnp.float32), dcache_all)
        )
        dquery_parts.append(dquery_block.reshape(extent, -1))
    return (jnp.concatenate(dquery_parts, axis=0).astype(jnp.bfloat16), dcache_all)


def feed_forward(shard_rows, gain_col, weight_pair, weight_down):
    full_rows = widen(shard_rows)
    inverse, normed = normalize(full_rows, gain_col)
    paired = jnp.einsum("td,djf->tjf", normed, weight_pair, preferred_element_type=jnp.float32)
    gate = paired[:, 0]
    upward = paired[:, 1]
    hidden = (jax.nn.silu(gate) * upward).astype(jnp.bfloat16)
    branch = jnp.einsum("tf,df->td", hidden, weight_down, preferred_element_type=jnp.float32)
    return (shard_rows + narrow(branch), (full_rows, inverse, normed, gate, upward, hidden))


def feed_backward(gradient, gain_col, weight_pair, weight_down, saved):
    full_rows, inverse, normed, gate, upward, hidden = saved
    dbranch = widen_grad(gradient)
    grad_down = jnp.einsum("td,tf->df", dbranch, hidden, preferred_element_type=jnp.float32)
    dhidden = jnp.einsum("td,df->tf", dbranch, weight_down, preferred_element_type=jnp.float32)
    sigma = jax.nn.sigmoid(gate)
    dgate = dhidden * upward * sigma * (1.0 + gate * (1.0 - sigma))
    dupward = dhidden * gate * sigma
    dpaired = jnp.stack([dgate, dupward], axis=1).astype(jnp.bfloat16)
    grad_pair = jnp.einsum("td,tjf->djf", normed, dpaired, preferred_element_type=jnp.float32)
    dnormed = jnp.einsum("tjf,djf->td", dpaired, weight_pair, preferred_element_type=jnp.float32)
    dfull, grad_gain = norm_back(full_rows, inverse, gain_col, dnormed)
    return (gradient + narrow(dfull), grad_pair, grad_down, grad_gain)


def shards(inputs, cotangent, proj_in, proj_out, ffn_in, ffn_down, gains):
    weight_in, weight_out, weight_ffn, weight_down, weight_gain = (
        lax.all_gather(proj_in, "seq", axis=0, tiled=True),
        lax.all_gather(proj_out, "seq", axis=0, tiled=True),
        lax.all_gather(ffn_in, "seq", axis=0, tiled=True),
        lax.all_gather(ffn_down, "seq", axis=0, tiled=True),
        lax.all_gather(gains, "seq", axis=0, tiled=True),
    )
    local_rows = inputs.shape[0]
    extent = min(512, local_rows)
    offset_pos = lax.axis_index("seq") * local_rows
    query_pos = offset_pos + jnp.arange(local_rows, dtype=jnp.int32)
    near_pos = offset_pos - local_rows + jnp.arange(2 * local_rows, dtype=jnp.int32)
    near_spans = [
        (offset, extent, local_rows + offset - WINDOW, WINDOW + extent)
        for offset in range(0, local_rows, extent)
    ]
    full0 = widen(inputs)
    inverse1, normed1 = normalize(full0, weight_gain[:, 0])
    own_qkv = jnp.einsum(
        "td,djc->tjc", normed1, weight_in[:, 0:3], preferred_element_type=jnp.float32
    ).astype(jnp.bfloat16)
    earlier = shifted(own_qkv[:, 1:3], "seq", 1)
    near_pairs = jnp.concatenate([earlier, own_qkv[:, 1:3]], axis=0)
    attended1, stats1 = attention_forward(
        own_qkv[:, 0], near_pairs, query_pos, near_pos, WINDOW, near_spans
    )
    state1 = inputs + narrow(
        jnp.einsum("tc,dc->td", attended1, weight_out[:, 0], preferred_element_type=jnp.float32)
    )
    state2, saved2 = feed_forward(state1, weight_gain[:, 1], weight_ffn[:, 0:2], weight_down[:, 0])
    full2 = widen(state2)
    inverse3, normed3 = normalize(full2, weight_gain[:, 2])
    inverse4, normed4 = normalize(full2, weight_gain[:, 3])
    local_cache = jnp.einsum(
        "td,djc->tjc", normed3, weight_in[:, 3:5], preferred_element_type=jnp.float32
    ).astype(jnp.bfloat16)
    query2 = jnp.einsum(
        "td,dc->tc", normed4, weight_in[:, 5], preferred_element_type=jnp.float32
    ).astype(jnp.bfloat16)
    cache_kv = lax.all_gather(local_cache, "seq", axis=0, tiled=True)
    attended2, stats2 = far_forward(query2, cache_kv, query_pos, extent)
    state3 = state2 + narrow(
        jnp.einsum("tc,dc->td", attended2, weight_out[:, 1], preferred_element_type=jnp.float32)
    )
    output, saved4 = feed_forward(state3, weight_gain[:, 4], weight_ffn[:, 2:4], weight_down[:, 1])
    weight_in, weight_out, weight_ffn, weight_down, weight_gain = (
        lax.all_gather(proj_in, "seq", axis=0, tiled=True),
        lax.all_gather(proj_out, "seq", axis=0, tiled=True),
        lax.all_gather(ffn_in, "seq", axis=0, tiled=True),
        lax.all_gather(ffn_down, "seq", axis=0, tiled=True),
        lax.all_gather(gains, "seq", axis=0, tiled=True),
    )
    grad3, grad_ffn2, grad_down2, grad_gain4 = feed_backward(
        cotangent, weight_gain[:, 4], weight_ffn[:, 2:4], weight_down[:, 1], saved4
    )
    dbranch2 = widen_grad(grad3)
    grad_out2 = jnp.einsum("td,tc->dc", dbranch2, attended2, preferred_element_type=jnp.float32)
    dattended2 = jnp.einsum(
        "td,dc->tc", dbranch2, weight_out[:, 1], preferred_element_type=jnp.float32
    ).astype(jnp.bfloat16)
    dquery2, dcache_all = far_backward(query2, cache_kv, query_pos, extent, stats2, dattended2)
    dcache = lax.psum_scatter(
        dcache_all.astype(jnp.bfloat16), "seq", scatter_dimension=0, tiled=True
    )
    grad_cache = jnp.einsum("td,tjc->djc", normed3, dcache, preferred_element_type=jnp.float32)
    grad_query2 = jnp.einsum("td,tc->dc", normed4, dquery2, preferred_element_type=jnp.float32)
    dnormed3 = jnp.einsum(
        "tjc,djc->td", dcache, weight_in[:, 3:5], preferred_element_type=jnp.float32
    )
    dnormed4 = jnp.einsum("tc,dc->td", dquery2, weight_in[:, 5], preferred_element_type=jnp.float32)
    dfull3, grad_gain2 = norm_back(full2, inverse3, weight_gain[:, 2], dnormed3)
    dfull4, grad_gain3 = norm_back(full2, inverse4, weight_gain[:, 3], dnormed4)
    grad2 = grad3 + narrow(dfull3 + dfull4)
    cross_in = jnp.concatenate([grad_cache, grad_query2[:, None]], axis=1)
    cross_gains = jnp.stack([grad_gain2, grad_gain3, grad_gain4], axis=1)
    grad1, grad_ffn1, grad_down1, grad_gain1 = feed_backward(
        grad2, weight_gain[:, 1], weight_ffn[:, 0:2], weight_down[:, 0], saved2
    )
    dbranch1 = widen_grad(grad1)
    grad_out1 = jnp.einsum("td,tc->dc", dbranch1, attended1, preferred_element_type=jnp.float32)
    dattended1 = jnp.einsum(
        "td,dc->tc", dbranch1, weight_out[:, 0], preferred_element_type=jnp.float32
    ).astype(jnp.bfloat16)
    dquery1, dnear = attention_backward(
        own_qkv[:, 0], near_pairs, query_pos, near_pos, WINDOW, near_spans, stats1, dattended1
    )
    returned = shifted(dnear[:local_rows].astype(jnp.bfloat16), "seq", -1).astype(jnp.float32)
    dqkv = jnp.concatenate(
        [dquery1[:, None], (dnear[local_rows:] + returned).astype(jnp.bfloat16)], axis=1
    )
    grad_self_in = jnp.einsum("td,tjc->djc", normed1, dqkv, preferred_element_type=jnp.float32)
    dnormed1 = jnp.einsum(
        "tjc,djc->td", dqkv, weight_in[:, 0:3], preferred_element_type=jnp.float32
    )
    dfull1, grad_gain0 = norm_back(full0, inverse1, weight_gain[:, 0], dnormed1)
    grad_inputs = grad1 + narrow(dfull1)
    self_gains = jnp.stack([grad_gain0, grad_gain1], axis=1)
    all_in = jnp.concatenate([grad_self_in, cross_in], axis=1)
    all_out = jnp.stack([grad_out1, grad_out2], axis=1)
    all_ffn = jnp.concatenate([grad_ffn1, grad_ffn2], axis=1)
    all_down = jnp.stack([grad_down1, grad_down2], axis=1)
    all_gains = jnp.concatenate([self_gains, cross_gains], axis=1)
    summed_in, summed_out, summed_ffn, summed_down, summed_gains = (
        lax.psum_scatter(
            all_in.astype(jnp.bfloat16), "seq", scatter_dimension=0, tiled=True
        ).astype(jnp.float32),
        lax.psum_scatter(
            all_out.astype(jnp.bfloat16), "seq", scatter_dimension=0, tiled=True
        ).astype(jnp.float32),
        lax.psum_scatter(
            all_ffn.astype(jnp.bfloat16), "seq", scatter_dimension=0, tiled=True
        ).astype(jnp.float32),
        lax.psum_scatter(
            all_down.astype(jnp.bfloat16), "seq", scatter_dimension=0, tiled=True
        ).astype(jnp.float32),
        lax.psum_scatter(
            all_gains.astype(jnp.bfloat16), "seq", scatter_dimension=0, tiled=True
        ).astype(jnp.float32),
    )
    total_gains = lax.psum(summed_gains, "tensor")
    return (output, grad_inputs, summed_in, summed_out, summed_ffn, summed_down, total_gains)


def solution(mesh):
    in_specs = (
        P("seq", "tensor"),
        P("seq", "tensor"),
        P("seq", None, "tensor"),
        P("seq", None, "tensor"),
        P("seq", None, "tensor"),
        P("seq", None, "tensor"),
        P("seq", None),
    )
    out_specs = (
        P("seq", "tensor"),
        P("seq", "tensor"),
        P("seq", None, "tensor"),
        P("seq", None, "tensor"),
        P("seq", None, "tensor"),
        P("seq", None, "tensor"),
        P("seq", None),
    )
    return jax.shard_map(shards, mesh=mesh, in_specs=in_specs, out_specs=out_specs, check_vma=False)
```

profile of v0, /device:TPU:28, one launch (start us, length us, event | category | flops | bytes accessed | tf_op | source)
XLA Modules:
  0.0 3295.7 jit_solution(5820022023264360410)
XLA Ops:
  21.5 68.0 %all-gather.14.cloned.1.call-done = bf16[1024,2048]{1,0:T(8,128)(2,1)} async-done(((bf16[1024,512]{1,0:T(8,128)(2,1)}), bf16[1024,2048]{1,0:T(8,128)(2,1)}) %all-gather.14.cloned.1.call-update) | async-done | bytes 4194320 | tf_op jit(solution)/shard_map/all_gather | solution.py:21
  93.1 73.4 %all-gather.16.cloned.1.call-done = bf16[2048,6,512]{0,2,1:T(8,128)(2,1)} async-done(((bf16[256,6,512]{0,2,1:T(8,128)(2,1)}), bf16[2048,6,512]{0,2,1:T(8,128)(2,1)}) %all-gather.16.cloned.1.call-update) | async-done | bytes 12582928 | tf_op jit(solution)/shard_map/all_gather | solution.py:273
  263.6 78.1 %reduce-scatter.15.cloned.1.call-done = bf16[1024,512]{1,0:T(8,128)(2,1)} async-done(((bf16[1024,2048]{1,0:T(8,128)(2,1)}), bf16[1024,512]{1,0:T(8,128)(2,1)}) %reduce-scatter.15.cloned.1.call-update) | async-done | bytes 1048592 | tf_op jit(solution)/shard_map/reduce_scatter | solution.py:31
  345.7 78.1 %all-gather.20.cloned.1.call-done = bf16[1024,2048]{1,0:T(8,128)(2,1)} async-done(((bf16[1024,512]{1,0:T(8,128)(2,1)}), bf16[1024,2048]{1,0:T(8,128)(2,1)}) %all-gather.20.cloned.1.call-update) | async-done | bytes 4194320 | tf_op jit(solution)/shard_map/all_gather | solution.py:21
  427.4 117.0 %all-gather.22.cloned.1.call-done = bf16[2048,4,1376]{0,2,1:T(8,128)(2,1)} async-done(((bf16[256,4,1376]{0,2,1:T(8,128)(2,1)}), bf16[2048,4,1376]{0,2,1:T(8,128)(2,1)}) %all-gather.22.cloned.1.call-update) | async-done | bytes 22544400 | tf_op jit(solution)/shard_map/all_gather | solution.py:275
  629.4 76.9 %reduce-scatter.17.cloned.1.call-done = bf16[1024,512]{1,0:T(8,128)(2,1)} async-done(((bf16[1024,2048]{1,0:T(8,128)(2,1)}), bf16[1024,512]{1,0:T(8,128)(2,1)}) %reduce-scatter.17.cloned.1.call-update) | async-done | bytes 1048592 | tf_op jit(solution)/shard_map/reduce_scatter | solution.py:31
  709.0 79.4 %all-gather.26.cloned.1.call-done = bf16[1024,2048]{1,0:T(8,128)(2,1)} async-done(((bf16[1024,512]{1,0:T(8,128)(2,1)}), bf16[1024,2048]{1,0:T(8,128)(2,1)}) %all-gather.26.cloned.1.call-update) | async-done | bytes 4194320 | tf_op jit(solution)/shard_map/all_gather | solution.py:21
  817.8 73.1 %all-gather.28.cloned.1.call-done = bf16[8192,2,512]{2,0,1:T(8,128)(2,1)} async-done(((bf16[1024,2,512]{2,0,1:T(8,128)(2,1)}), bf16[8192,2,512]{2,0,1:T(8,128)(2,1)}) %all-gather.28.cloned.1.call-update) | async-done | bytes 16777232 | tf_op jit(solution)/shard_map/all_gather | solution.py:311
  948.5 74.2 %while.109 = (s32[]{:T(128)}, f32[512,4,128]{0,2,1:T(8,128)}, s32[]{:T(128)}, bf16[8192,2,512]{0,2,1:T(8,128)(2,1)}, s32[512]{0:T(512)S(1)}, /*index=5*/bf16[512...) while((s32[]{:T(128)}, f32[512,4,128]{0,2,1:T(8,128)}, ...), condition=%wide.region_20.21_spmd, body=%wide.region_19.20_spmd.sunk | while | flops 544475136 | bytes 6321351 | solution.py:178
  1058.8 63.6 %while.107 = (s32[]{:T(128)}, f32[512,4,128]{0,2,1:T(8,128)}, s32[]{:T(128)}, bf16[8192,2,512]{0,2,1:T(8,128)(2,1)}, s32[512]{0:T(512)S(1)}, /*index=5*/bf16[512...) while((s32[]{:T(128)}, f32[512,4,128]{0,2,1:T(8,128)}, ...), condition=%wide.region_14.15_spmd, body=%wide.region_13.14_spmd.sunk | while | flops 544475136 | bytes 6321351 | solution.py:178
  1130.1 206.5 %reduce-scatter.19.cloned.1.call-done = bf16[1024,512]{1,0:T(8,128)(2,1)} async-done(((bf16[1024,2048]{1,0:T(8,128)(2,1)}), bf16[1024,512]{1,0:T(8,128)(2,1)}) %reduce-scatter.19.cloned.1.call-update) | async-done | bytes 1048592 | tf_op jit(solution)/shard_map/reduce_scatter | solution.py:31
  1342.9 76.6 %all-gather.30.cloned.1.call-done = bf16[1024,2048]{1,0:T(8,128)(2,1)} async-done(((bf16[1024,512]{1,0:T(8,128)(2,1)}), bf16[1024,2048]{1,0:T(8,128)(2,1)}) %all-gather.30.cloned.1.call-update) | async-done | bytes 4194320 | tf_op jit(solution)/shard_map/all_gather | solution.py:21
  1440.0 61.1 %all-gather.32.cloned.1.call-done = bf16[1024,2048]{1,0:T(8,128)(2,1)} async-done(((bf16[1024,512]{1,0:T(8,128)(2,1)}), bf16[1024,2048]{1,0:T(8,128)(2,1)}) %all-gather.32.cloned.1.call-update) | async-done | bytes 4194320 | tf_op jit(solution)/shard_map/all_gather | solution.py:27
  1538.6 77.4 %reduce-scatter.23.cloned.1.call-done = bf16[1024,512]{1,0:T(8,128)(2,1)} async-done(((bf16[1024,2048]{1,0:T(8,128)(2,1)}), bf16[1024,512]{1,0:T(8,128)(2,1)}) %reduce-scatter.23.cloned.1.call-update) | async-done | bytes 1048592 | tf_op jit(solution)/shard_map/reduce_scatter | solution.py:31
  1618.6 79.4 %all-gather.34.cloned.1.call-done = bf16[1024,2048]{1,0:T(8,128)(2,1)} async-done(((bf16[1024,512]{1,0:T(8,128)(2,1)}), bf16[1024,2048]{1,0:T(8,128)(2,1)}) %all-gather.34.cloned.1.call-update) | async-done | bytes 4194320 | tf_op jit(solution)/shard_map/all_gather | solution.py:27
  1796.6 86.9 %while.111 = (s32[]{:T(128)}, f32[512,4,128]{0,2,1:T(8,128)S(1)}, f32[8192,2,512]{0,2,1:T(8,128)}, s32[]{:T(128)}, bf16[8192,2,512]{0,2,1:T(8,128)(2,1)}, /*inde...) while((s32[]{:T(128)}, f32[512,4,128]{0,2,1:T(8,128)S(1)}, ...), condition=%wide.region_30.31_spmd, body=%wide.region_29.30_spmd.sunk | while | flops 1354500096 | bytes 35689696 | solution.py:238
  1883.6 97.0 %while.113 = (s32[]{:T(128)}, f32[512,4,128]{0,2,1:T(8,128)S(1)}, f32[8192,2,512]{0,2,1:T(8,128)}, s32[]{:T(128)}, bf16[8192,2,512]{0,2,1:T(8,128)(2,1)}, /*inde...) while((s32[]{:T(128)}, f32[512,4,128]{0,2,1:T(8,128)S(1)}, ...), condition=%wide.region_35.36_spmd, body=%wide.region_34.35_spmd.sunk | while | flops 1354500096 | bytes 35689696 | solution.py:238
  1998.1 283.5 %reduce-scatter.25.cloned.1.call-done = bf16[1024,2,512]{0,2,1:T(8,128)(2,1)} async-done(((bf16[8192,2,512]{0,2,1:T(8,128)(2,1)}), bf16[1024,2,512]{0,2,1:T(8,128)(2,1)}) %reduce-scatter.25.cloned.1.call-update) | async-done | bytes 2097168 | tf_op jit(solution)/shard_map/reduce_scatter | solution.py:333
  2300.8 76.5 %reduce-scatter.27.cloned.1.call-done = bf16[1024,512]{1,0:T(8,128)(2,1)} async-done(((bf16[1024,2048]{1,0:T(8,128)(2,1)}), bf16[1024,512]{1,0:T(8,128)(2,1)}) %reduce-scatter.27.cloned.1.call-update) | async-done | bytes 1048592 | tf_op jit(solution)/shard_map/reduce_scatter | solution.py:31
  2380.1 79.2 %all-gather.36.cloned.1.call-done = bf16[1024,2048]{1,0:T(8,128)(2,1)} async-done(((bf16[1024,512]{1,0:T(8,128)(2,1)}), bf16[1024,2048]{1,0:T(8,128)(2,1)}) %all-gather.36.cloned.1.call-update) | async-done | bytes 4194320 | tf_op jit(solution)/shard_map/all_gather | solution.py:27
  2499.9 77.4 %reduce-scatter.29.cloned.1.call-done = bf16[1024,512]{1,0:T(8,128)(2,1)} async-done(((bf16[1024,2048]{1,0:T(8,128)(2,1)}), bf16[1024,512]{1,0:T(8,128)(2,1)}) %reduce-scatter.29.cloned.1.call-update) | async-done | bytes 1048592 | tf_op jit(solution)/shard_map/reduce_scatter | solution.py:31
  2964.7 76.6 %reduce-scatter.31.cloned.1.call-done = bf16[1024,512]{1,0:T(8,128)(2,1)} async-done(((bf16[1024,2048]{1,0:T(8,128)(2,1)}), bf16[1024,512]{1,0:T(8,128)(2,1)}) %reduce-scatter.31.cloned.1.call-update) | async-done | bytes 1048592 | tf_op jit(solution)/shard_map/reduce_scatter | solution.py:31
  3045.2 144.3 %reduce-scatter.37.cloned.1.call-done = bf16[256,4,1376]{0,2,1:T(8,128)(2,1)} async-done(((bf16[2048,4,1376]{0,2,1:T(8,128)(2,1)}), bf16[256,4,1376]{0,2,1:T(8,128)(2,1)}) %reduce-scatter.37.cloned.1.call-update) | async-done | bytes 2818064 | tf_op jit(solution)/shard_map/reduce_scatter | solution.py:381
  3194.2 91.0 %reduce-scatter.33.cloned.1.call-done = bf16[256,6,512]{2,0,1:T(8,128)(2,1)} async-done(((bf16[2048,6,512]{2,0,1:T(8,128)(2,1)}), bf16[256,6,512]{2,0,1:T(8,128)(2,1)}) %reduce-scatter.33.cloned.1.call-update) | async-done | bytes 1572880 | tf_op jit(solution)/shard_map/reduce_scatter | solution.py:375
  (1016 shorter events, 1445.8 us)
Async XLA Ops:
  11.7 245.1 %all-gather.18.cloned.1.call-start = ((), (), s32[]{:S(2)}) async-start(), calls=%async_computation.16 | async-start | bytes 4718592 | tf_op jit(solution)/shard_map/all_gather | solution.py:274
  181.7 160.1 %reduce-scatter.15.cloned.1.call-start = ((), (), s32[]{:S(2)}) async-start(), calls=%async_computation.17 | async-start | bytes 5242880 | tf_op jit(solution)/shard_map/reduce_scatter | solution.py:31
  263.6 160.2 %all-gather.20.cloned.1.call-start = ((), (), s32[]{:S(2)}) async-start(), calls=%async_computation.18 | async-start | bytes 5242880 | tf_op jit(solution)/shard_map/all_gather | solution.py:21
  344.3 200.1 %all-gather.22.cloned.1.call-start = ((), (), s32[]{:S(2)}) async-start(), calls=%async_computation.19 | async-start | bytes 25362432 | tf_op jit(solution)/shard_map/all_gather | solution.py:275
  344.9 270.4 %all-gather.24.cloned.1.call-start = ((), (), s32[]{:S(2)}) async-start(), calls=%async_computation.20 | async-start | bytes 12681216 | tf_op jit(solution)/shard_map/all_gather | solution.py:276
  345.6 360.7 %reduce-scatter.17.cloned.1.call-start = ((), (), s32[]{:S(2)}) async-start(), calls=%async_computation.21 | async-start | bytes 5242880 | tf_op jit(solution)/shard_map/reduce_scatter | solution.py:31
  629.0 159.4 %all-gather.26.cloned.1.call-start = ((), (), s32[]{:S(2)}) async-start(), calls=%async_computation.22 | async-start | bytes 5242880 | tf_op jit(solution)/shard_map/all_gather | solution.py:21
  709.0 181.9 %all-gather.28.cloned.1.call-start = ((), (), s32[]{:S(2)}) async-start(), calls=%async_computation.23 | async-start | bytes 18874368 | tf_op jit(solution)/shard_map/all_gather | solution.py:311
  800.6 536.1 %reduce-scatter.19.cloned.1.call-start = ((), (), s32[]{:S(2)}) async-start(), calls=%async_computation.24 | async-start | bytes 5242880 | tf_op jit(solution)/shard_map/reduce_scatter | solution.py:31
  1130.1 289.5 %all-gather.30.cloned.1.call-start = ((), (), s32[]{:S(2)}) async-start(), calls=%async_computation.25 | async-start | bytes 5242880 | tf_op jit(solution)/shard_map/all_gather | solution.py:21
  1340.1 161.0 %all-gather.32.cloned.1.call-start = ((), (), s32[]{:S(2)}) async-start(), calls=%async_computation.27 | async-start | bytes 5242880 | tf_op jit(solution)/shard_map/all_gather | solution.py:27
  1342.8 273.2 %reduce-scatter.23.cloned.1.call-start = ((), (), s32[]{:S(2)}) async-start(), calls=%async_computation.28 | async-start | bytes 5242880 | tf_op jit(solution)/shard_map/reduce_scatter | solution.py:31
  1538.6 159.4 %all-gather.34.cloned.1.call-start = ((), (), s32[]{:S(2)}) async-start(), calls=%async_computation.29 | async-start | bytes 5242880 | tf_op jit(solution)/shard_map/all_gather | solution.py:27
  1618.6 663.1 %reduce-scatter.25.cloned.1.call-start = ((), (), s32[]{:S(2)}) async-start(), calls=%async_computation.30 | async-start | bytes 18874368 | tf_op jit(solution)/shard_map/reduce_scatter | solution.py:333
  1997.9 379.3 %reduce-scatter.27.cloned.1.call-start = ((), (), s32[]{:S(2)}) async-start(), calls=%async_computation.31 | async-start | bytes 5242880 | tf_op jit(solution)/shard_map/reduce_scatter | solution.py:31
  2300.7 158.6 %all-gather.36.cloned.1.call-start = ((), (), s32[]{:S(2)}) async-start(), calls=%async_computation.32 | async-start | bytes 5242880 | tf_op jit(solution)/shard_map/all_gather | solution.py:27
  2379.9 197.4 %reduce-scatter.29.cloned.1.call-start = ((), (), s32[]{:S(2)}) async-start(), calls=%async_computation.33 | async-start | bytes 5242880 | tf_op jit(solution)/shard_map/reduce_scatter | solution.py:31
  2499.8 160.0 %all-gather.38.cloned.1.call-start = ((), (), s32[]{:S(2)}) async-start(), calls=%async_computation.34 | async-start | bytes 5242880 | tf_op jit(solution)/shard_map/all_gather | solution.py:27
  2580.4 316.3 %reduce-scatter.21.cloned.1.call-start = ((), (), s32[]{:S(2)}) async-start(), calls=%async_computation.26 | async-start | bytes 5242880 | tf_op jit(solution)/shard_map/reduce_scatter | solution.py:31
  2594.9 307.6 %reduce-scatter.41.cloned.1.call-start = ((), (), s32[]{:S(2)}) async-start(), calls=%async_computation.40 | async-start | bytes 36864 | tf_op jit(solution)/shard_map/reduce_scatter | solution.py:387
  2795.3 166.9 %reduce-scatter.35.cloned.1.call-start = ((), (), s32[]{:S(2)}) async-start(), calls=%async_computation.37 | async-start | bytes 4718592 | tf_op jit(solution)/shard_map/reduce_scatter | solution.py:378
  2806.1 235.2 %reduce-scatter.31.cloned.1.call-start = ((), (), s32[]{:S(2)}) async-start(), calls=%async_computation.35 | async-start | bytes 5242880 | tf_op jit(solution)/shard_map/reduce_scatter | solution.py:31
  2813.8 375.7 %reduce-scatter.37.cloned.1.call-start = ((), (), s32[]{:S(2)}) async-start(), calls=%async_computation.38 | async-start | bytes 25362432 | tf_op jit(solution)/shard_map/reduce_scatter | solution.py:381
  2869.8 415.3 %reduce-scatter.33.cloned.1.call-start = ((), (), s32[]{:S(2)}) async-start(), calls=%async_computation.36 | async-start | bytes 14155776 | tf_op jit(solution)/shard_map/reduce_scatter | solution.py:375
  (115 other events, 6562.0 us)
Sparse Core Ops, SparseCore 0:
  10.2 79.1 all-gather.13
  91.9 74.6 all-gather.15
  263.7 77.9 reduce-scatter.14
  344.4 79.2 all-gather.19
  425.6 118.7 all-gather.21
  546.5 68.7 all-gather.23
  629.1 77.1 reduce-scatter.16
  709.1 79.2 all-gather.25
  800.7 90.1 all-gather.27
  1130.2 206.4 reduce-scatter.18
  1340.2 79.2 all-gather.29
  1421.7 79.2 all-gather.31
  1538.7 77.2 reduce-scatter.22
  1618.7 79.2 all-gather.33
  1998.0 283.6 reduce-scatter.24
  2300.8 76.3 reduce-scatter.26
  2380.0 79.2 all-gather.35
  2500.0 77.2 reduce-scatter.28
  2580.5 79.2 all-gather.37
  2662.1 77.2 reduce-scatter.20
  2821.9 85.2 reduce-scatter.38
  2965.0 76.2 reduce-scatter.30
  3045.4 144.0 reduce-scatter.36
  3192.8 92.3 reduce-scatter.32
  (3 shorter events, 127.5 us)
where the time goes:
time: 3310 us; the launch traced here: 3300 us
  waiting for transfers between devices  2160 us (65%)
  matrix products  613 us (19%)
  other arithmetic  280 us (8%)
  local copies, waits for them, and re-layouts  185 us (6%)
    reduce_scatter x8, waiting for transfers between devices, narrow(): lax.psum_scatter(partial_value.astype(jnp.bfloat16), 'tensor', scatter_di...  669 us
    all_gather x4, waiting for transfers between devices, widen(): lax.all_gather(shard_rows.astype(jnp.bfloat16), 'tensor', axis=1, tiled=T...  302 us
    reduce_scatter x1, waiting for transfers between devices, shards(): lax.psum_scatter(dcache_all.astype(jnp.bfloat16), 'seq', scatter_dimensio...  284 us
    all_gather x4, waiting for transfers between devices, widen_grad(): lax.all_gather(shard_rows.astype(jnp.bfloat16), 'tensor', axis=1, tiled=T...  272 us
    reduce_scatter x1, waiting for transfers between devices, shards(): lax.psum_scatter(all_ffn.astype(jnp.bfloat16), 'seq', scatter_dimension=0...  144 us
    all_gather x1, waiting for transfers between devices, shards(): lax.all_gather(ffn_in, 'seq', axis=0, tiled=True)  117 us
    reduce_scatter x1, waiting for transfers between devices, shards(): lax.psum_scatter(all_in.astype(jnp.bfloat16), 'seq', scatter_dimension=0,...  91 us
    dot_general x19, matrix products, value_step(): jnp.einsum('hrk,khe->rhe', probability, value_rows, preferred_element_typ...  90 us
  transfers between devices with their start and end apart: 29, of which 25 were waited for; matrix products, arithmetic and copies ran while one was open for 11% of the time, Pallas kernels for 0%

commit v1 on v0

v1 whole, which is shorter than its diff:
```python
import functools

import jax
import jax.numpy as jnp
from jax import lax
from jax.experimental import pallas as pl
from jax.experimental.pallas import tpu as pltpu
from jax.sharding import PartitionSpec as P

HEAD_DIM = 128
WINDOW = 1024
SCALE = HEAD_DIM ** (-0.5)
SCALE2 = SCALE * 1.4426950408889634

epsilon = 1e-06
floor_score = -1e30
f32 = jnp.float32
bf16 = jnp.bfloat16
MIB = 1 << 20


def nt(left, right):
    return lax.dot_general(left, right, (((1,), (1,)), ((), ())), preferred_element_type=f32)


def tn(left, right):
    return lax.dot_general(left, right, (((0,), (0,)), ((), ())), preferred_element_type=f32)


def nn(left, right):
    return lax.dot_general(left, right, (((1,), (0,)), ((), ())), preferred_element_type=f32)


def row_dot(dout, out):
    product = dout.astype(f32) * out.astype(f32)
    return jnp.sum(product.T, axis=0, keepdims=True)


def near_allowed(span, size, start, rows):
    key = lax.broadcasted_iota(jnp.int32, (span, size), 0)
    query = lax.broadcasted_iota(jnp.int32, (span, size), 1)
    first = jnp.where(lax.axis_index("seq") == 0, rows - start, 0)
    return (key >= jnp.maximum(query + 1, first)) & (key <= query + WINDOW)


def near_forward_kernel(rows, q_ref, k_ref, v_ref, o_ref, stat_ref):
    size = q_ref.shape[0]
    span = WINDOW + size
    start = pl.multiple_of(pl.program_id(1) * size + (rows - WINDOW), size)
    allowed = near_allowed(span, size, start, rows)
    scores = nt(k_ref[pl.ds(start, span), :], q_ref[...]) * SCALE2
    scores = jnp.where(allowed, scores, floor_score)
    top = jnp.max(scores, axis=0, keepdims=True)
    weight = jnp.exp2(scores - top)
    total = jnp.sum(weight, axis=0, keepdims=True)
    mixed = tn(v_ref[pl.ds(start, span), :], weight.astype(bf16)) / total
    o_ref[...] = mixed.T.astype(bf16)
    stat_ref[0] = top + jnp.log2(total)


def near_forward(queries, keys, values):
    rows, width = queries.shape
    heads, size = width // HEAD_DIM, min(256, rows)
    own = pl.BlockSpec((size, HEAD_DIM), lambda h, b: (b, h))
    span = pl.BlockSpec((keys.shape[0], HEAD_DIM), lambda h, b: (0, h))
    stat = pl.BlockSpec((1, 1, size), lambda h, b: (h, 0, b))
    pairs = heads * rows * (WINDOW + size)
    return pl.pallas_call(
        functools.partial(near_forward_kernel, rows),
        grid=(heads, rows // size),
        in_specs=[own, span, span],
        out_specs=[own, stat],
        out_shape=[
            jax.ShapeDtypeStruct((rows, width), bf16),
            jax.ShapeDtypeStruct((heads, 1, rows), f32),
        ],
        compiler_params=pltpu.CompilerParams(vmem_limit_bytes=40 * MIB),
        cost_estimate=pl.CostEstimate(
            flops=pairs * 4 * HEAD_DIM * 2, bytes_accessed=rows * width * 12, transcendentals=pairs
        ),
        name="near_forward",
    )(queries, keys, values)


def near_backward_kernel(rows, q_ref, k_ref, v_ref, do_ref, o_ref, stat_ref, dq_ref, dk_ref, dv_ref):
    size = q_ref.shape[0]
    span = WINDOW + size
    start = pl.multiple_of(pl.program_id(1) * size + (rows - WINDOW), size)

    @pl.when(pl.program_id(1) == 0)
    def clear():
        dk_ref[...] = jnp.zeros_like(dk_ref)
        dv_ref[...] = jnp.zeros_like(dv_ref)

    place = pl.ds(start, span)
    queries, dout = q_ref[...], do_ref[...]
    keys, values = k_ref[place, :], v_ref[place, :]
    inner = row_dot(dout, o_ref[...])
    allowed = near_allowed(span, size, start, rows)
    scores = nt(keys, queries) * SCALE2 - stat_ref[0]
    weight = jnp.exp2(jnp.where(allowed, scores, floor_score))
    dscore = (weight * (nt(values, dout) - inner)).astype(bf16)
    dv_ref[place, :] += nn(weight.astype(bf16), dout)
    dk_ref[place, :] += nn(dscore, queries) * SCALE
    dq_ref[...] = (tn(keys, dscore) * SCALE).T.astype(bf16)


def near_backward(queries, keys, values, dresult, result, stats):
    rows, width = queries.shape
    heads, size = width // HEAD_DIM, min(256, rows)
    own = pl.BlockSpec((size, HEAD_DIM), lambda h, b: (b, h))
    span = pl.BlockSpec((keys.shape[0], HEAD_DIM), lambda h, b: (0, h))
    stat = pl.BlockSpec((1, 1, size), lambda h, b: (h, 0, b))
    pairs = heads * rows * (WINDOW + size)
    return pl.pallas_call(
        functools.partial(near_backward_kernel, rows),
        grid=(heads, rows // size),
        in_specs=[own, span, span, own, own, stat],
        out_specs=[own, span, span],
        out_shape=[
            jax.ShapeDtypeStruct((rows, width), bf16),
            jax.ShapeDtypeStruct(keys.shape, f32),
            jax.ShapeDtypeStruct(keys.shape, f32),
        ],
        compiler_params=pltpu.CompilerParams(vmem_limit_bytes=40 * MIB),
        cost_estimate=pl.CostEstimate(
            flops=pairs * 10 * HEAD_DIM * 2, bytes_accessed=rows * width * 32, transcendentals=pairs
        ),
        name="near_backward",
    )(queries, keys, values, dresult, result, stats)


def far_place(block):
    mine, count = lax.axis_index("seq"), lax.axis_size("seq")
    return jnp.where(block == 0, 2 * mine, 2 * count - 1 - 2 * mine)


def triangle(size, start, width):
    key = lax.broadcasted_iota(jnp.int32, (size, width), 0)
    query = lax.broadcasted_iota(jnp.int32, (size, width), 1)
    return key <= query + start


def query_parts(size):
    return [(start, size // 2) for start in (0, size // 2)]


def far_forward_kernel(q_ref, kv_ref, o_ref, stat_ref, top_ref, sum_ref, acc_ref):
    size = q_ref.shape[0]
    last = far_place(pl.program_id(1))
    top_ref[...] = jnp.full_like(top_ref, floor_score)
    sum_ref[...] = jnp.zeros_like(sum_ref)
    acc_ref[...] = jnp.zeros_like(acc_ref)

    def step(index, masked):
        place = pl.ds(pl.multiple_of(index * size, size), size)
        keys, values = kv_ref[place, :HEAD_DIM], kv_ref[place, HEAD_DIM:]
        parts = query_parts(size)
        all_scores = [nt(keys, q_ref[start : start + width, :]) for start, width in parts]
        for (start, width), scores in zip(parts, all_scores):
            own = slice(start, start + width)
            scores = scores * SCALE2
            if masked:
                scores = jnp.where(triangle(size, start, width), scores, floor_score)
            before = top_ref[:, own]
            top = jnp.maximum(before, jnp.max(scores, axis=0, keepdims=True))
            weight = jnp.exp2(scores - top)
            fade = jnp.exp2(before - top)
            top_ref[:, own] = top
            sum_ref[:, own] = sum_ref[:, own] * fade + jnp.sum(weight, axis=0, keepdims=True)
            acc_ref[:, own] = acc_ref[:, own] * fade + tn(values, weight.astype(bf16))

    @pl.loop(0, last)
    def earlier(index):
        step(index, False)

    step(last, True)
    o_ref[...] = (acc_ref[...] / sum_ref[...]).T.astype(bf16)
    stat_ref[0] = top_ref[...] + jnp.log2(sum_ref[...])


def far_forward(queries, pairs_kv):
    rows, width = queries.shape
    heads, size = width // HEAD_DIM, rows // 2
    own = pl.BlockSpec((size, HEAD_DIM), lambda h, b: (b, h))
    whole = pl.BlockSpec((pairs_kv.shape[0], 2 * HEAD_DIM), lambda h, b: (0, h))
    stat = pl.BlockSpec((1, 1, size), lambda h, b: (h, 0, b))
    pairs = heads * rows * pairs_kv.shape[0] // 2
    return pl.pallas_call(
        far_forward_kernel,
        grid=(heads, 2),
        in_specs=[own, whole],
        out_specs=[own, stat],
        out_shape=[
            jax.ShapeDtypeStruct((rows, width), bf16),
            jax.ShapeDtypeStruct((heads, 1, rows), f32),
        ],
        scratch_shapes=[
            pltpu.VMEM((1, size), f32),
            pltpu.VMEM((1, size), f32),
            pltpu.VMEM((HEAD_DIM, size), f32),
        ],
        compiler_params=pltpu.CompilerParams(vmem_limit_bytes=48 * MIB),
        cost_estimate=pl.CostEstimate(
            flops=pairs * 4 * HEAD_DIM * 2,
            bytes_accessed=pairs_kv.shape[0] * width * 4,
            transcendentals=pairs,
        ),
        name="far_forward",
    )(queries, pairs_kv)


def far_backward_kernel(
    q_ref, kv_ref, do_ref, o_ref, stat_ref, dq_ref, dkv_ref, dq_acc, dk_acc, dv_acc
):
    size = q_ref.shape[0]
    block = pl.program_id(1)
    last = far_place(block)

    @pl.when(block == 0)
    def clear():
        dk_acc[...] = jnp.zeros_like(dk_acc)
        dv_acc[...] = jnp.zeros_like(dv_acc)

    dq_acc[...] = jnp.zeros_like(dq_acc)
    inner = row_dot(do_ref[...], o_ref[...])

    def step(index, masked):
        place = pl.ds(pl.multiple_of(index * size, size), size)
        keys, values = kv_ref[place, :HEAD_DIM], kv_ref[place, HEAD_DIM:]
        parts = []
        for start, width in query_parts(size):
            own = slice(start, start + width)
            queries, dout = q_ref[own, :], do_ref[own, :]
            parts.append((start, width, own, queries, dout, nt(keys, queries), nt(values, dout)))
        dvalues, dkeys = [], []
        for start, width, own, queries, dout, scores, dweight in parts:
            scores = scores * SCALE2 - stat_ref[0, :, own]
            if masked:
                scores = jnp.where(triangle(size, start, width), scores, floor_score)
            weight = jnp.exp2(scores)
            dscore = (weight * (dweight - inner[:, own])).astype(bf16)
            dvalues.append(nn(weight.astype(bf16), dout))
            dkeys.append(nn(dscore, queries))
            dq_acc[:, own] += tn(keys, dscore)
        dv_acc[place, :] += dvalues[0] + dvalues[1]
        dk_acc[place, :] += dkeys[0] + dkeys[1]

    @pl.loop(0, last)
    def earlier(index):
        step(index, False)

    step(last, True)
    dq_ref[...] = (dq_acc[...] * SCALE).T.astype(bf16)

    @pl.when(block == 1)
    def leave():
        dkv_ref[:, :HEAD_DIM] = (dk_acc[...] * SCALE).astype(bf16)
        dkv_ref[:, HEAD_DIM:] = dv_acc[...].astype(bf16)


def far_backward(queries, pairs_kv, dresult, result, stats):
    rows, width = queries.shape
    heads, size = width // HEAD_DIM, rows // 2
    tokens = pairs_kv.shape[0]
    own = pl.BlockSpec((size, HEAD_DIM), lambda h, b: (b, h))
    whole = pl.BlockSpec((tokens, 2 * HEAD_DIM), lambda h, b: (0, h))
    stat = pl.BlockSpec((1, 1, size), lambda h, b: (h, 0, b))
    pairs = heads * rows * tokens // 2
    return pl.pallas_call(
        far_backward_kernel,
        grid=(heads, 2),
        in_specs=[own, whole, own, own, stat],
        out_specs=[own, whole],
        out_shape=[
            jax.ShapeDtypeStruct((rows, width), bf16),
            jax.ShapeDtypeStruct(pairs_kv.shape, bf16),
        ],
        scratch_shapes=[
            pltpu.VMEM((HEAD_DIM, size), f32),
            pltpu.VMEM((tokens, HEAD_DIM), f32),
            pltpu.VMEM((tokens, HEAD_DIM), f32),
        ],
        compiler_params=pltpu.CompilerParams(vmem_limit_bytes=60 * MIB),
        cost_estimate=pl.CostEstimate(
            flops=pairs * 10 * HEAD_DIM * 2,
            bytes_accessed=tokens * width * 8,
            transcendentals=pairs,
        ),
        name="far_backward",
    )(queries, pairs_kv, dresult, result, stats)


def greet_neighbours(mine, count, partner=None):
    barrier = pltpu.get_barrier_semaphore()
    sides = ((-1, mine > 0), (1, mine < count - 1))
    if partner is not None:
        pl.semaphore_signal(
            barrier, inc=1, device_id={"seq": partner}, device_id_type=pl.DeviceIdType.MESH
        )
    for side, present in sides:

        @pl.when(present)
        def greet():
            pl.semaphore_signal(
                barrier,
                inc=1,
                device_id={"tensor": mine + side},
                device_id_type=pl.DeviceIdType.MESH,
            )

    others = 0 if partner is None else 1
    pl.semaphore_wait(barrier, others + sum(present.astype(jnp.int32) for _, present in sides))


def chain_kernel(chunk, turns, own_only, part_ref, base_ref, *refs):
    if own_only:
        own_ref, out_ref, *refs = refs
    else:
        out_ref, *refs = refs
    sum_ref, rs_send, rs_recv, ag_send, ag_recv, *refs = refs
    turn = refs[0] if turns else None
    count = lax.axis_size("tensor")
    mine = lax.axis_index("tensor")
    rows, depth = part_ref.shape
    half, pieces, slack = depth // 2, rows // chunk, 2
    hops = count // 2 - 1 if own_only else count - 1
    ticks = pieces + slack * (count - 1 + hops)
    core = lax.rem(lax.axis_index("seq"), 2)
    partner = lax.axis_index("seq") + 1 - 2 * core if turns else None
    greet_neighbours(mine, count, partner)
    if turns:

        @pl.when(core == 1)
        def follow():
            pl.semaphore_wait(turn, 1)

    flows = [(0, mine, -1), (1, count - 1 - mine, 1)]

    def area(flow, piece):
        return (pl.ds(pl.multiple_of(piece * chunk, chunk), chunk), pl.ds(flow * half, half))

    def inward(flow, step, piece, source):
        rows_cols = area(flow, piece)
        return pltpu.make_async_remote_copy(
            src_ref=source.at[rows_cols],
            dst_ref=sum_ref.at[rows_cols],
            send_sem=rs_send.at[flow, piece],
            recv_sem=rs_recv.at[flow, piece],
            device_id={"tensor": mine + step},
            device_id_type=pl.DeviceIdType.MESH,
        )

    def outward(flow, step, piece, hop):
        rows_cols = area(flow, piece)
        if own_only:
            width = depth // count
            start, length = (hop + 1) * width, half - (hop + 1) * width
            rows_cols = (rows_cols[0], pl.ds(half if flow else start, length))
        return pltpu.make_async_remote_copy(
            src_ref=out_ref.at[rows_cols],
            dst_ref=out_ref.at[rows_cols],
            send_sem=ag_send.at[flow, piece],
            recv_sem=ag_recv.at[flow, piece],
            device_id={"tensor": mine - step},
            device_id_type=pl.DeviceIdType.MESH,
        )

    @pl.loop(0, ticks)
    def beat(tick):
        if turns:

            @pl.when((core == 0) & (tick == ticks * 7 // 8))
            def lead():
                pl.semaphore_signal(
                    turn, inc=1, device_id={"seq": partner}, device_id_type=pl.DeviceIdType.MESH
                )

        for flow, far, step in flows:
            piece = tick - slack * (count - 1 - far)
            live = (piece >= 0) & (piece < pieces)

            @pl.when(live & (far == count - 1))
            def leaf():
                inward(flow, step, piece, part_ref).start()

            @pl.when(live & (far < count - 1))
            def arrived():
                inward(flow, step, piece, sum_ref).wait_recv()

            @pl.when(live & (far < count - 1) & (far > 0))
            def middle():
                rows_cols = area(flow, piece)
                sum_ref[rows_cols] = (
                    sum_ref[rows_cols].astype(f32) + part_ref[rows_cols].astype(f32)
                ).astype(bf16)
                inward(flow, step, piece, sum_ref).start()

            @pl.when(live & (far == 0))
            def root():
                rows_cols = area(flow, piece)
                out_ref[rows_cols] = (
                    sum_ref[rows_cols].astype(f32)
                    + part_ref[rows_cols].astype(f32)
                    + base_ref[rows_cols].astype(f32)
                ).astype(bf16)
                if hops > 0:
                    outward(flow, step, piece, 0).start()

        for flow, far, step in flows:
            piece = tick - slack * (count - 1 + far)
            live = (piece >= 0) & (piece < pieces)
            for hop in range(hops) if own_only else (0,):

                @pl.when(live & ((far == hop + 1) if own_only else (far > 0)))
                def landed():
                    outward(flow, step, piece, hop).wait_recv()

                if own_only and hop + 1 == hops:
                    continue

                @pl.when(live & ((far == hop + 1) if own_only else (far > 0) & (far < hops)))
                def forward():
                    outward(flow, step, piece, hop + 1).start()

    if own_only:
        width = depth // count
        own_ref[...] = out_ref[:, pl.ds(pl.multiple_of(mine * width, width), width)].astype(f32)

    @pl.loop(0, pieces)
    def finish(piece):
        for flow, far, step in flows:

            @pl.when(far > 0)
            def sent_in():
                inward(flow, step, piece, sum_ref).wait_send()

            for hop in range(hops) if own_only else (0,):

                @pl.when((far == hop) if own_only else (far < hops))
                def sent_out():
                    outward(flow, step, piece, hop).wait_send()


def chain_sum(partial_value, base, turns=0, own_only=False):
    turns = turns if lax.axis_size("seq") % 2 == 0 else 0
    rows, depth = base.shape
    chunk = 32
    pieces = rows // chunk
    own_width = depth // lax.axis_size("tensor") if own_only else depth
    whole = pl.BlockSpec(memory_space=pltpu.VMEM)
    return pl.pallas_call(
        functools.partial(chain_kernel, chunk, turns, own_only),
        in_specs=[whole, whole],
        out_specs=whole,
        out_shape=jax.ShapeDtypeStruct((rows, own_width), f32 if own_only else bf16),
        scratch_shapes=[pltpu.VMEM((rows, depth), bf16)] * (2 if own_only else 1)
        + [pltpu.SemaphoreType.DMA((2, pieces))] * 4
        + [pltpu.SemaphoreType.REGULAR] * (turns > 0),
        compiler_params=pltpu.CompilerParams(
            collective_id=1 + turns if turns else 6 * own_only, has_side_effects=True, vmem_limit_bytes=32 * MIB
        ),
        cost_estimate=pl.CostEstimate(
            flops=10**11, bytes_accessed=rows * depth * 6, transcendentals=0
        ),
        name="chain_sum_turns" if turns else "chain_own" if own_only else "chain_sum",
    )(partial_value.astype(bf16), base)


def spread_kernel(chunk, own_ref, out_ref, send_sem, recv_sem):
    count = lax.axis_size("tensor")
    mine = lax.axis_index("tensor")
    rows, width = own_ref.shape
    pieces = rows // chunk
    greet_neighbours(mine, count)

    def copy(way, side, hop, piece):
        source = jnp.clip(mine - side * hop, 0, count - 1)
        place = (
            pl.ds(pl.multiple_of(piece * chunk, chunk), chunk),
            pl.ds(pl.multiple_of(source * width, width), width),
        )
        return pltpu.make_async_remote_copy(
            src_ref=out_ref.at[place],
            dst_ref=out_ref.at[place],
            send_sem=send_sem.at[way, hop, piece],
            recv_sem=recv_sem.at[way, hop, piece],
            device_id={"tensor": jnp.clip(mine + side, 0, count - 1)},
            device_id_type=pl.DeviceIdType.MESH,
        )

    def landing(way, side, hop, piece):
        source = jnp.clip(mine - side * hop, 0, count - 1)
        place = (
            pl.ds(pl.multiple_of(piece * chunk, chunk), chunk),
            pl.ds(pl.multiple_of(source * width, width), width),
        )
        return pltpu.make_async_remote_copy(
            src_ref=out_ref.at[place],
            dst_ref=out_ref.at[place],
            send_sem=send_sem.at[way, hop - 1, piece],
            recv_sem=recv_sem.at[way, hop - 1, piece],
            device_id={"tensor": jnp.clip(mine + side, 0, count - 1)},
            device_id_type=pl.DeviceIdType.MESH,
        )

    ways = [(0, 1), (1, -1)]
    out_ref[:, pl.ds(pl.multiple_of(mine * width, width), width)] = own_ref[...].astype(bf16)

    for hop in range(count):

        @pl.loop(0, pieces)
        def pass_on(piece):
            for way, side in ways:
                source, target = mine - side * hop, mine + side
                held = (source >= 0) & (source < count)

                if hop > 0:

                    @pl.when(held)
                    def landed():
                        landing(way, side, hop, piece).wait_recv()

                if hop < count - 1:

                    @pl.when(held & (target >= 0) & (target < count))
                    def forward():
                        copy(way, side, hop, piece).start()

    for hop in range(count - 1):

        @pl.loop(0, pieces)
        def finish(piece):
            for way, side in ways:
                source, target = mine - side * hop, mine + side

                @pl.when((source >= 0) & (source < count) & (target >= 0) & (target < count))
                def sent():
                    copy(way, side, hop, piece).wait_send()


def spread(own_rows):
    rows, width = own_rows.shape
    count, chunk = lax.axis_size("tensor"), 128
    whole = pl.BlockSpec(memory_space=pltpu.VMEM)
    return pl.pallas_call(
        functools.partial(spread_kernel, chunk),
        in_specs=[whole],
        out_specs=whole,
        out_shape=jax.ShapeDtypeStruct((rows, width * count), bf16),
        scratch_shapes=[pltpu.SemaphoreType.DMA((2, count - 1, rows // chunk))] * 2,
        compiler_params=pltpu.CompilerParams(
            collective_id=1, has_side_effects=True, vmem_limit_bytes=24 * MIB
        ),
        cost_estimate=pl.CostEstimate(
            flops=7 * 10**10, bytes_accessed=rows * width * 20, transcendentals=0
        ),
        name="spread",
    )(own_rows)


def small_kernel(own_ref, out_ref, land_ref, send_sem, recv_sem):
    count = lax.axis_size("tensor")
    mine = lax.axis_index("tensor")
    barrier = pltpu.get_barrier_semaphore()
    others = [lax.rem(mine + step, count) for step in range(1, count)]
    for other in others:
        pl.semaphore_signal(
            barrier, inc=1, device_id={"tensor": other}, device_id_type=pl.DeviceIdType.MESH
        )
    pl.semaphore_wait(barrier, count - 1)
    copies = [
        pltpu.make_async_remote_copy(
            src_ref=own_ref,
            dst_ref=land_ref.at[mine],
            send_sem=send_sem.at[slot],
            recv_sem=recv_sem.at[slot],
            device_id={"tensor": other},
            device_id_type=pl.DeviceIdType.MESH,
        )
        for slot, other in enumerate(others)
    ]
    for copy in copies:
        copy.start()
    land_ref[mine] = own_ref[...]
    for copy in copies:
        copy.wait()
    total = land_ref[0]
    for place in range(1, count):
        total = total + land_ref[place]
    out_ref[...] = total


def small_sum(value):
    count = lax.axis_size("tensor")
    whole = pl.BlockSpec(memory_space=pltpu.VMEM)
    return pl.pallas_call(
        small_kernel,
        in_specs=[whole],
        out_specs=whole,
        out_shape=jax.ShapeDtypeStruct(value.shape, f32),
        scratch_shapes=[pltpu.VMEM((count, *value.shape), f32)]
        + [pltpu.SemaphoreType.DMA((count - 1,))] * 2,
        compiler_params=pltpu.CompilerParams(collective_id=5, has_side_effects=True),
        cost_estimate=pl.CostEstimate(flops=10**9, bytes_accessed=value.size * 8, transcendentals=0),
        name="small_sum",
    )(value)


def shifted(block, axis, distance):
    devices = range(lax.axis_size(axis))
    route = [(i - distance, i) for i in devices if i - distance in devices]
    return lax.ppermute(block, axis, route)


def swapped(block):
    count, half = lax.axis_size("seq"), block.shape[0] // 2
    other = lax.ppermute(block[half:], "seq", [(i, count - 1 - i) for i in range(count)])
    return jnp.concatenate([block[:half], other], axis=0)


def gathered(weight):
    return lax.all_gather(weight, "seq", axis=0, tiled=True)


def scattered(grad):
    return lax.psum_scatter(grad.astype(bf16), "seq", scatter_dimension=0, tiled=True)


def together(value, grads):
    return lax.optimization_barrier((value.astype(bf16), tuple(g.astype(bf16) for g in grads)))


def inverse_rms(rows):
    return lax.rsqrt(jnp.mean(rows * rows, axis=1, keepdims=True) + epsilon)


def norm_back(rows, gain_row, gradient):
    inverse = inverse_rms(rows)
    scaled = gradient * gain_row
    cubed = inverse * inverse * inverse
    dfull = inverse * scaled - rows * cubed * jnp.mean(scaled * rows, axis=1, keepdims=True)
    return (dfull, jnp.sum(gradient * rows * inverse, axis=0, keepdims=True))


def row_block(size, width):
    return pl.BlockSpec((size, width), lambda i: (i, 0))


def resident(array):
    return pl.BlockSpec(array.shape, lambda i: (0, 0), pipeline_mode=pl.Buffered(1))


def blocks_call(kernel, name, rows, size, ins, outs, flops, weights=()):
    in_specs = [row_block(size, x.shape[1]) if cut else resident(x) for x, cut in ins]
    in_specs += [pl.BlockSpec(memory_space=pl.ANY) for _ in weights]
    scratch = [pltpu.VMEM(x.shape, x.dtype) for x in weights]
    if weights:
        scratch.append(pltpu.SemaphoreType.DMA((3,)))
    out_specs = [
        row_block(size, shape[1]) if cut else pl.BlockSpec(shape, lambda i: (0, 0))
        for shape, _, cut in outs
    ]
    return pl.pallas_call(
        kernel,
        grid=(rows // size,),
        in_specs=in_specs,
        out_specs=out_specs,
        out_shape=[jax.ShapeDtypeStruct(shape, kind) for shape, kind, _ in outs],
        compiler_params=pltpu.CompilerParams(vmem_limit_bytes=56 * MIB),
        cost_estimate=pl.CostEstimate(
            flops=flops, bytes_accessed=sum(x.size * 2 for x, _ in ins), transcendentals=0
        ),
        scratch_shapes=scratch,
        name=name,
    )(*[x for x, _ in ins], *weights)


def project_kernel(parts, full_ref, weight_ref, *refs):
    gains, outs = refs[: len(parts)], refs[len(parts) :]
    rows = full_ref[...].astype(f32)
    scaled = rows * inverse_rms(rows)
    for place, (start, width) in enumerate(parts):
        normed = (scaled * gains[place][...]).astype(bf16)
        outs[2 * place][...] = normed
        outs[2 * place + 1][...] = nn(normed, weight_ref[:, start : start + width]).astype(bf16)


def project(full, weight, parts):
    rows, depth = full.shape
    outs = []
    for _, _, width in parts:
        outs += [((rows, depth), bf16, True), ((rows, width), bf16, True)]
    return blocks_call(
        functools.partial(project_kernel, [part[1:] for part in parts]),
        "project",
        rows,
        min(256, rows),
        [(full, True), (weight, False)] + [(gain, False) for gain, _, _ in parts],
        outs,
        2 * rows * depth * sum(width for _, _, width in parts),
    )


def project_back_kernel(parts, full_ref, weight_ref, *refs):
    count = len(parts)
    gains, grads, dfull_ref, dgains = refs[:count], refs[count : 2 * count], refs[2 * count], refs[2 * count + 1 :]

    @pl.when(pl.program_id(0) == 0)
    def clear():
        for ref in dgains:
            ref[...] = jnp.zeros_like(ref)

    rows = full_ref[...].astype(f32)
    total = jnp.zeros_like(rows)
    for place, (start, width) in enumerate(parts):
        dnormed = nt(grads[place][...], weight_ref[:, start : start + width])
        dfull, dgain = norm_back(rows, gains[place][...], dnormed)
        total = total + dfull
        dgains[place][...] += dgain
    dfull_ref[...] = total.astype(bf16)


def project_back(full, weight, parts):
    rows, depth = full.shape
    return blocks_call(
        functools.partial(project_back_kernel, [part[1:3] for part in parts]),
        "project_back",
        rows,
        min(256, rows),
        [(full, True), (weight, False)]
        + [(part[0], False) for part in parts]
        + [(part[3], True) for part in parts],
        [((rows, depth), bf16, True)] + [((1, depth), f32, False)] * len(parts),
        2 * rows * depth * sum(part[2] for part in parts),
    )


def weight_copies(pair_hbm, down_hbm, pair_weight, down_weight, sems):
    half = down_weight.shape[1]
    gate, upward = pl.ds(0, half), pl.ds(half, half)
    return [
        pltpu.make_async_copy(pair_hbm.at[:, gate], pair_weight.at[:, gate], sems.at[0]),
        pltpu.make_async_copy(pair_hbm.at[:, upward], pair_weight.at[:, upward], sems.at[1]),
        pltpu.make_async_copy(down_hbm, down_weight, sems.at[2]),
    ]


def at_first(action):
    pl.when(pl.program_id(0) == 0)(action)


def feed_forward_kernel(
    full_ref, gain_ref, pair_hbm, down_hbm, branch_ref, normed_ref, pair_ref, hidden_ref, *weights
):
    pair_weight, down_weight, sems = weights
    copies = weight_copies(pair_hbm, down_hbm, pair_weight, down_weight, sems)
    half = hidden_ref.shape[1]

    @at_first
    def fetch():
        for copy in copies:
            copy.start()

    rows = full_ref[...].astype(f32)
    normed = (rows * inverse_rms(rows) * gain_ref[...]).astype(bf16)
    normed_ref[...] = normed
    at_first(copies[0].wait)
    gate = nn(normed, pair_weight[:, :half])
    at_first(copies[1].wait)
    upward = nn(normed, pair_weight[:, half:])
    pair_ref[:, :half] = gate.astype(bf16)
    pair_ref[:, half:] = upward.astype(bf16)
    hidden = (gate * jax.nn.sigmoid(gate) * upward).astype(bf16)
    hidden_ref[...] = hidden
    at_first(copies[2].wait)
    branch_ref[...] = nt(hidden, down_weight[...]).astype(bf16)


def feed_forward(full, gain, weight_pair, weight_down):
    rows, depth = full.shape
    half = weight_down.shape[1]
    branch, normed, pair, hidden = blocks_call(
        feed_forward_kernel,
        "feed_forward",
        rows,
        min(512, rows),
        [(full, True), (gain, False)],
        [
            ((rows, depth), bf16, True),
            ((rows, depth), bf16, True),
            ((rows, 2 * half), bf16, True),
            ((rows, half), bf16, True),
        ],
        6 * rows * depth * half,
        (weight_pair, weight_down),
    )
    return (branch, (full, normed, pair, hidden))


def feed_backward_kernel(
    dout_ref, full_ref, pair_ref, gain_ref, pair_hbm, down_hbm, dfull_ref, dpair_ref, dgain_ref, *weights
):
    pair_weight, down_weight, sems = weights
    copies = weight_copies(pair_hbm, down_hbm, pair_weight, down_weight, sems)
    half = down_weight.shape[1]

    @at_first
    def fetch():
        for copy in copies[::-1]:
            copy.start()
        dgain_ref[...] = jnp.zeros_like(dgain_ref)
        copies[2].wait()

    dhidden = nn(dout_ref[...], down_weight[...])
    gate, upward = pair_ref[:, :half].astype(f32), pair_ref[:, half:].astype(f32)
    sigma = jax.nn.sigmoid(gate)
    dpair_ref[:, :half] = (dhidden * upward * sigma * (1.0 + gate * (1.0 - sigma))).astype(bf16)
    dpair_ref[:, half:] = (dhidden * gate * sigma).astype(bf16)

    @at_first
    def have_pair():
        copies[0].wait()
        copies[1].wait()

    dfull, dgain = norm_back(
        full_ref[...].astype(f32), gain_ref[...], nt(dpair_ref[...], pair_weight[...])
    )
    dfull_ref[...] = dfull.astype(bf16)
    dgain_ref[...] += dgain


def feed_backward(dbranch, gain, weight_pair, weight_down, saved):
    full, normed, pair, hidden = saved
    rows, depth = full.shape
    half = weight_down.shape[1]
    dfull, dpair, grad_gain = blocks_call(
        feed_backward_kernel,
        "feed_backward",
        rows,
        min(512, rows),
        [
            (dbranch, True),
            (full, True),
            (pair, True),
            (gain, False),
        ],
        [((rows, depth), bf16, True), ((rows, 2 * half), bf16, True), ((1, depth), f32, False)],
        6 * rows * depth * half,
        (weight_pair, weight_down),
    )
    return (dfull, [(normed, dpair), (dbranch, hidden)], grad_gain)


def gradients_kernel(count, *refs):
    lefts, rights, extra, out_ref = refs[:count], refs[count : 2 * count], refs[2 * count : -1], refs[-1]
    start = 0
    for left, right in zip(lefts, rights):
        width = right.shape[1]
        out_ref[:, start : start + width] = tn(left[...], right[...]).astype(bf16)
        start += width
    for ref in extra:
        out_ref[:, start : start + ref.shape[1]] = ref[...]
        start += ref.shape[1]


def gradients(pairs, extra=()):
    rows, depth = pairs[0][0].shape
    size = min(512, depth)
    total = sum(right.shape[1] for _, right in pairs) + sum(x.shape[1] for x in extra)
    return pl.pallas_call(
        functools.partial(gradients_kernel, len(pairs)),
        grid=(depth // size,),
        in_specs=[pl.BlockSpec((rows, size), lambda i: (0, i)) for _ in pairs]
        + [resident(right) for _, right in pairs]
        + [row_block(size, x.shape[1]) for x in extra],
        out_specs=row_block(size, total),
        out_shape=jax.ShapeDtypeStruct((depth, total), bf16),
        compiler_params=pltpu.CompilerParams(vmem_limit_bytes=56 * MIB),
        cost_estimate=pl.CostEstimate(
            flops=2 * rows * depth * total, bytes_accessed=depth * total * 4, transcendentals=0
        ),
        name="gradients",
    )(*[left for left, _ in pairs], *[right for _, right in pairs], *extra)


def padded(width):
    return -(-width // 128) * 128


def pad_columns(weight):
    width = weight.shape[1]
    return jnp.pad(weight, ((0, 0), (0, padded(width) - width)))


def shards(inputs, cotangent, proj_in, proj_out, ffn_in, ffn_down, gains):
    rows = inputs.shape[0]
    width = proj_in.shape[2]
    depth = proj_in.shape[0]
    heads = width // HEAD_DIM
    hidden_width = ffn_down.shape[2]
    half = padded(hidden_width)
    packed = gathered(
        jnp.concatenate([proj_in[:, 0:3].reshape(depth, 3 * width), pad_columns(gains)], axis=1)
    )
    gain_rows = nt(jnp.eye(8, 5, dtype=bf16), packed[:, 3 * width : 3 * width + 5])
    gain = [gain_rows[j : j + 1] for j in range(5)]
    full0 = spread(inputs)
    w_out1 = gathered(proj_out[:, 0])
    own_pair1 = jnp.concatenate([pad_columns(ffn_in[:, j]) for j in (0, 1)], axis=1)
    own_pair2 = jnp.concatenate([pad_columns(ffn_in[:, j]) for j in (2, 3)], axis=1)
    cache_in = proj_in[:, 3:5].reshape(depth, 2, heads, HEAD_DIM).transpose(0, 2, 1, 3)
    own_cross = jnp.concatenate([cache_in.reshape(depth, 2 * width), proj_in[:, 5]], axis=1)

    normed1, own = project(full0, packed, [(gain[0], 0, 3 * width)])
    query1 = own[:, :width]
    earlier = shifted(own[:, width:], "seq", 1)
    earlier, own_pair1, own_down1 = lax.optimization_barrier(
        (earlier, own_pair1, ffn_down[:, 0])
    )
    w_pair1 = gathered(own_pair1)
    w_down1 = gathered(pad_columns(own_down1))
    w_cross = gathered(own_cross)
    w_out2 = gathered(proj_out[:, 1])
    near = jnp.concatenate([earlier, own[:, width:]], axis=0)
    key1, value1 = near[:, :width], near[:, width:]
    attended1, stats1 = near_forward(query1, key1, value1)
    full1 = chain_sum(nt(attended1, w_out1), full0, turns=1)
    branch1, saved1 = feed_forward(full1, gain[1], w_pair1, w_down1)
    full2 = chain_sum(branch1, full1)
    normed3, local_cache, normed4, query2 = project(
        full2, w_cross, [(gain[2], 0, 2 * width), (gain[3], 2 * width, width)]
    )
    local_cache, own_dout, w_out2, own_down2 = lax.optimization_barrier(
        (local_cache, cotangent, w_out2, ffn_down[:, 1])
    )
    cache_kv = gathered(local_cache)
    dfull4 = spread(own_dout)
    query2 = swapped(query2)
    query2, dfull4 = lax.optimization_barrier((query2, dfull4))
    w_down2 = gathered(pad_columns(own_down2))
    attended2, stats2 = far_forward(query2, cache_kv)
    own_attended2 = swapped(attended2)
    own_attended2, own_pair2 = lax.optimization_barrier((own_attended2, own_pair2))
    w_pair2 = gathered(own_pair2)
    full3 = chain_sum(nt(own_attended2, w_out2), full2, turns=2)
    branch2, saved2 = feed_forward(full3, gain[4], w_pair2, w_down2)

    dpart, pairs_feed2, grad_gain4 = feed_backward(dfull4, gain[4], w_pair2, w_down2, saved2)
    dfull3 = chain_sum(dpart, dfull4)
    dattended2 = swapped(nn(dfull3, w_out2).astype(bf16))
    dquery2, dcache = far_backward(query2, cache_kv, dattended2, attended2, stats2)
    dcache, branch2, pairs_feed2 = lax.optimization_barrier((dcache, branch2, pairs_feed2))
    dquery2 = swapped(dquery2)
    dcache = lax.psum_scatter(dcache, "seq", scatter_dimension=0, tiled=True)
    output = chain_sum(branch2, full3, own_only=True)
    grad_feed2 = gradients(pairs_feed2)
    dcache, output, grad_feed2 = lax.optimization_barrier((dcache, output, grad_feed2))
    grad_feed2 = scattered(grad_feed2)
    dpart, grad_gain2, grad_gain3 = project_back(
        full2,
        w_cross,
        [(gain[2], 0, 2 * width, dcache), (gain[3], 2 * width, width, dquery2)],
    )
    dpart, (grad_cross,) = together(
        dpart,
        (gradients([(normed3, dcache), (normed4, dquery2), (dfull3, own_attended2)]),),
    )
    grad_cross = scattered(grad_cross)
    dfull2 = chain_sum(dpart, dfull3, turns=3)
    dpart, pairs_feed1, grad_gain1 = feed_backward(dfull2, gain[1], w_pair1, w_down1, saved1)
    dpart, (grad_feed1,) = together(dpart, (gradients(pairs_feed1),))
    grad_feed1 = scattered(grad_feed1)
    dpart, grad_cross, grad_feed2 = lax.optimization_barrier((dpart, grad_cross, grad_feed2))
    dfull1 = chain_sum(dpart, dfull2)
    dattended1 = nn(dfull1, w_out1).astype(bf16)
    dquery1, dkey1, dvalue1 = near_backward(query1, key1, value1, dattended1, attended1, stats1)
    dnear = jnp.concatenate([dkey1, dvalue1], axis=1)
    returned = shifted(dnear[:rows].astype(bf16), "seq", -1).astype(f32)
    grad_first = gradients([(normed1, dquery1), (dfull1, attended1)])
    dpairs = (dnear[rows:] + returned).astype(bf16)
    dself = jnp.concatenate([dquery1, dpairs], axis=1)
    dself, grad_feed1 = lax.optimization_barrier((dself, grad_feed1))
    dpart, grad_gain0 = project_back(full0, packed, [(gain[0], 0, 3 * width, dself)])
    all_gains = [grad_gain0, grad_gain1, grad_gain2, grad_gain3, grad_gain4]
    all_gains = pad_columns(jnp.concatenate(all_gains, axis=0).T.astype(bf16))
    dpart, (grad_self,) = together(
        dpart, (gradients([(normed1, dself[:, width:])], (grad_first, all_gains)),)
    )
    grad_self = scattered(grad_self)
    grad_inputs, grad_self = lax.optimization_barrier(
        (chain_sum(dpart, dfull1, own_only=True), grad_self)
    )
    total_gains = small_sum(grad_self[:, 4 * width :].astype(f32))[:, :5]
    grad_cache = grad_cross[:, : 2 * width].reshape(depth, heads, 2, HEAD_DIM)
    grad_cache = grad_cache.transpose(0, 2, 1, 3).reshape(depth, 2 * width)
    grad_in = jnp.concatenate(
        [
            grad_self[:, 2 * width : 3 * width],
            grad_self[:, : 2 * width],
            grad_cache,
            grad_cross[:, 2 * width : 3 * width],
        ],
        axis=1,
    )
    grad_out = [grad_self[:, 3 * width : 4 * width], grad_cross[:, 3 * width :]]
    grad_ffn = [
        grads[:, start : start + hidden_width]
        for grads in (grad_feed1, grad_feed2)
        for start in (0, half)
    ]
    grad_down = [grads[:, 2 * half : 2 * half + hidden_width] for grads in (grad_feed1, grad_feed2)]
    return (
        output,
        grad_inputs,
        grad_in.astype(f32).reshape(depth, 6, width),
        jnp.stack(grad_out, axis=1).astype(f32),
        jnp.stack(grad_ffn, axis=1).astype(f32),
        jnp.stack(grad_down, axis=1).astype(f32),
        total_gains,
    )


def solution(mesh):
    wide = P("seq", "tensor")
    weight = P("seq", None, "tensor")
    gain = P("seq", None)
    return jax.shard_map(
        shards,
        mesh=mesh,
        in_specs=(wide, wide, weight, weight, weight, weight, gain),
        out_specs=(wide, wide, weight, weight, weight, weight, gain),
        check_vma=False,
    )
```

time: 3310 us -> 1620 us (0.49)
  waiting for transfers between devices: 2160 us -> 125 us
  Pallas kernels: 0 us -> 1220 us
  matrix products: 613 us -> 14.6 us
  other arithmetic: 280 us -> 29.1 us
  starting transfers between devices: 8.95 us -> 87 us
  local copies, waits for them, and re-layouts: 185 us -> 117 us
    pallas_call x0 -> x28, Pallas kernels: none -> 1220 us  [the longest x8 649 us: chain_sum(): pl.pallas_call(functools.partial(chain_kernel, chunk, turns, own_only), i...]
    reduce_scatter x14 -> x5, waiting for transfers between devices: 1230 us -> 54.2 us  [the longest x4 49.3 us: scattered(): lax.psum_scatter(grad.astype(bf16), 'seq', scatter_dimension=0, tiled=True)]
    all_gather x13 -> x9, waiting for transfers between devices: 891 us -> 17.4 us  [gathered(): return lax.all_gather(weight, 'seq', axis=0, tiled=True)]
    dot_general x208 -> x5, matrix products: 591 us -> 14.6 us  [the longest x3 9.96 us: nt(): lax.dot_general(left, right, (((1,), (1,)), ((), ())), preferred_element_...]
    slice x84 -> x18, local copies, waits for them, and re-layouts: 116 us -> 18.6 us  [the longest x1 3.35 us: shards(): ffn_in[:, j]]
    ppermute x0 -> x4, starting transfers between devices: none -> 82.6 us  [swapped(): lax.ppermute(block[half:], 'seq', [(i, count - 1 - i) for i in range(coun...]
    convert_element_type x20 -> x6, other arithmetic: 93 us -> 14.6 us  [the longest x1 5.23 us: shards(): jnp.stack(grad_ffn, axis=1).astype(f32)]
    dynamic_update_slice x19 -> x0, other arithmetic: 64.7 us -> none  [grad_step(): lax.dynamic_update_slice_in_dim(dcache_now, before + stacked, start, 0)]
  transfers between devices with their start and end apart: 29 -> 20, of which waited for: 25 -> 7; matrix products, arithmetic and copies ran while one was open for 11% -> 5% of each run, Pallas kernels for 0% -> 59%
where the time goes in v1:
time: 1620 us; the launch traced here: 1610 us
  Pallas kernels  1220 us (75%)
  waiting for transfers between devices  125 us (8%)
  local copies, waits for them, and re-layouts  117 us (7%)
  starting transfers between devices  87 us (5%)
  other arithmetic  29.1 us (2%)
    pallas_call x8, Pallas kernels, chain_sum(): pl.pallas_call(functools.partial(chain_kernel, chunk, turns, own_only), i...  649 us
    pallas_call x8, Pallas kernels, blocks_call(): pl.pallas_call(kernel, grid=(rows // size,), in_specs=in_specs, out_specs...  178 us
    pallas_call x2, Pallas kernels, spread(): pl.pallas_call(functools.partial(spread_kernel, chunk), in_specs=[whole],...  143 us
    pallas_call x5, Pallas kernels, gradients(): pl.pallas_call(functools.partial(gradients_kernel, len(pairs)), grid=(dep...  86.7 us
    ppermute x4, starting transfers between devices, swapped(): lax.ppermute(block[half:], 'seq', [(i, count - 1 - i) for i in range(coun...  82.6 us
    unnamed x134, local copies, waits for them, and re-layouts  78.9 us
    pallas_call x1, Pallas kernels, far_backward(): pl.pallas_call(far_backward_kernel, grid=(heads, 2), in_specs=[own, whole...  64.3 us
    reduce_scatter x4, waiting for transfers between devices, scattered(): lax.psum_scatter(grad.astype(bf16), 'seq', scatter_dimension=0, tiled=True)  49.3 us
  transfers between devices with their start and end apart: 20, of which 7 were waited for; matrix products, arithmetic and copies ran while one was open for 5% of the time, Pallas kernels for 59%

profile of v1, /device:TPU:28, one launch (start us, length us, event | category | flops | bytes accessed | tf_op | source)
XLA Modules:
  0.0 1610.5 jit_solution(2267882890170187075)
XLA Ops:
  13.2 70.9 %spread.2.full_ref.base_ref = bf16[1024,2048]{1,0:T(8,128)(2,1)S(1)} custom-call(f32[1024,512]{1,0:T(8,128)S(1)} %copy-done.12), custom_call_target="tpu_custom_call" | custom-call | flops 70000001024 | bytes 10485760 | tf_op jit(solution)/shard_map/spread/pallas_call | solution.py:546
  145.0 16.6 %near_forward.1 = (bf16[1024,512]{1,0:T(8,128)(2,1)S(1)}, f32[4,1,1024]{2,1,0:T(1,128)S(1)}) custom-call(bf16[1024,512]{1,0:T(8,128)(2,1)S(1)} %slice.143.q_ref, bf16[2048,512]{1,0:T(8,128)(2,1)S(1)} %get-tuple-element.163.k_ref, bf16[2048,512]{1,0:T(8,128)(2,1)S(1)} %get-tuple-element.162.v_ref), custom_call_target="tpu_custom_call" | custom-call | flops 5368709120 | bytes 6291456 | tf_op jit(solution)/shard_map/near_forward/pallas_call | solution.py:68
  168.7 74.1 %chain_sum_turns.3.full_ref.base_ref = bf16[1024,2048]{1,0:T(8,128)(2,1)S(1)} custom-call(bf16[1024,2048]{1,0:T(8,128)(2,1)S(1)} %convolution_convert_fusion.1.part_ref, bf16[1024,2048]{1,0:T(8,128)(2,1)S(1)} %copy-done.21), custom_call_target="tpu_custom_call" | custom-call | flops 99999997952 | bytes 12582912 | tf_op jit(solution)/shard_map/chain_sum_turns/pallas_call | solution.py:452
  244.8 27.7 %feed_forward.2 = (bf16[1024,2048]{1,0:T(8,128)(2,1)}, bf16[1024,2048]{1,0:T(8,128)(2,1)}, bf16[1024,2816]{1,0:T(8,128)(2,1)}, bf16[1024,1408]{1,0:T(8,128)(2,1)}) custom-call(bf16[1024,2048]{1,0:T(8,128)(2,1)} %copy-done.30, f32[1,2048]{1,0:T(1,128)} %get-tuple-element.193.gain_ref, bf16[2048,2816]{1,0:T(8,128)(2,1)} %all-gather.14.cloned.1.call-done.pair_hbm, ...), custom_call_target="tpu_custom_call" | custom-call | flops 17716740096 | bytes 4198400 | tf_op jit(solution)/shard_map/feed_forward/pallas_call | solution.py:664
  275.2 78.7 %chain_sum.3.full_ref.base_ref = bf16[1024,2048]{1,0:T(8,128)(2,1)S(1)} custom-call(bf16[1024,2048]{1,0:T(8,128)(2,1)S(1)} %copy-done.37, bf16[1024,2048]{1,0:T(8,128)(2,1)S(1)} %copy-done.31), custom_call_target="tpu_custom_call" | custom-call | flops 99999997952 | bytes 12582912 | tf_op jit(solution)/shard_map/chain_sum/pallas_call | solution.py:452
  370.8 42.0 %collective-permute-start.1 = (bf16[512,512]{1,0:T(8,128)(2,1)S(1)}, bf16[512,512]{1,0:T(8,128)(2,1)S(1)}, u32[]{:S(2)}, u32[]{:S(2)}) collective-permute-start(bf16[512,512]{1,0:T(8,128)(2,1)S(1)} %get-tuple-element.187), channel_id=1, source_target_pairs={{0,28},{4,24},{8,20},{12,16},{16,12},{20,8},{24,4},{28,0},{1,29},{... | collective-permute-start | bytes 1572872 | tf_op jit(solution)/shard_map/ppermute | solution.py:618
  412.8 71.7 %spread.3.dout_ref.base_ref.refs_1_ = bf16[1024,2048]{1,0:T(8,128)(2,1)S(1)} custom-call(f32[1024,512]{1,0:T(8,128)S(1)} %copy-done.13), custom_call_target="tpu_custom_call" | custom-call | flops 70000001024 | bytes 10485760 | tf_op jit(solution)/shard_map/spread/pallas_call | solution.py:546
  486.7 17.4 %all-gather.20.cloned.1.call-done.kv_ref = bf16[8192,1024]{1,0:T(8,128)(2,1)} async-done(((bf16[1024,1024]{1,0:T(8,128)(2,1)}), bf16[8192,1024]{1,0:T(8,128)(2,1)}) %all-gather.20.cloned.1.call-update) | async-done | bytes 16777232 | tf_op jit(solution)/shard_map/all_gather | solution.py:623
  504.1 48.6 %far_forward.1 = (bf16[1024,512]{1,0:T(8,128)(2,1)S(1)}, f32[4,1,1024]{2,1,0:T(1,128)S(1)}) custom-call(bf16[1024,512]{1,0:T(8,128)(2,1)S(1)} %pad_maximum_fusion.2.q_ref, bf16[8192,1024]{1,0:T(8,128)(2,1)} %all-gather.20.cloned.1.call-done.kv_ref), custom_call_target="tpu_custom_call" | custom-call | flops 17179869184 | bytes 16777216 | tf_op jit(solution)/shard_map/far_forward/pallas_call | solution.py:189
  575.0 75.1 %chain_sum_turns.4.full_ref.base_ref = bf16[1024,2048]{1,0:T(8,128)(2,1)S(1)} custom-call(bf16[1024,2048]{1,0:T(8,128)(2,1)S(1)} %convolution_convert_fusion.part_ref, bf16[1024,2048]{1,0:T(8,128)(2,1)S(1)} %copy-done.24), custom_call_target="tpu_custom_call" | custom-call | flops 99999997952 | bytes 12582912 | tf_op jit(solution)/shard_map/chain_sum_turns/pallas_call | solution.py:452
  652.1 27.5 %feed_forward.3 = (bf16[1024,2048]{1,0:T(8,128)(2,1)}, bf16[1024,2048]{1,0:T(8,128)(2,1)}, bf16[1024,2816]{1,0:T(8,128)(2,1)}, bf16[1024,1408]{1,0:T(8,128)(2,1)}) custom-call(bf16[1024,2048]{1,0:T(8,128)(2,1)} %copy-done.32, f32[1,2048]{1,0:T(1,128)} %get-tuple-element.190.gain_ref, bf16[2048,2816]{1,0:T(8,128)(2,1)} %all-gather.22.cloned.1.call-done.pair_hbm, ...), custom_call_target="tpu_custom_call" | custom-call | flops 17716740096 | bytes 4198400 | tf_op jit(solution)/shard_map/feed_forward/pallas_call | solution.py:664
  679.6 31.7 %feed_backward.2 = (bf16[1024,2048]{1,0:T(8,128)(2,1)}, bf16[1024,2816]{1,0:T(8,128)(2,1)}, f32[1,2048]{1,0:T(1,128)}) custom-call(bf16[1024,2048]{1,0:T(8,128)(2,1)} %copy-done.26, bf16[1024,2048]{1,0:T(8,128)(2,1)} %copy-done.32, bf16[1024,2816]{1,0:T(8,128)(2,1)} %get-tuple-element.91.pair_ref, f32[1,2048]{1,0:T(1,128)} %get-tuple-element.190.gain_ref, ...), custom_call_target="tpu_custom_call" | custom-call | flops 17716740096 | bytes 14159872 | tf_op jit(solution)/shard_map/feed_backward/pallas_call | solution.py:664
  713.5 81.4 %chain_sum.4.refs_2_.base_ref = bf16[1024,2048]{1,0:T(8,128)(2,1)S(1)} custom-call(bf16[1024,2048]{1,0:T(8,128)(2,1)S(1)} %copy-done.35, bf16[1024,2048]{1,0:T(8,128)(2,1)S(1)} %copy-done.27), custom_call_target="tpu_custom_call" | custom-call | flops 99999997952 | bytes 12582912 | tf_op jit(solution)/shard_map/chain_sum/pallas_call | solution.py:452
  797.3 37.9 %collective-permute-start.3 = (bf16[512,512]{1,0:T(8,128)(2,1)S(1)}, bf16[512,512]{1,0:T(8,128)(2,1)S(1)}, u32[]{:S(2)}, u32[]{:S(2)}) collective-permute-start(bf16[512,512]{1,0:T(8,128)(2,1)S(1)} %get-tuple-element.183), channel_id=1, source_target_pairs={{0,28},{4,24},{8,20},{12,16},{16,12},{20,8},{24,4},{28,0},{1,29},{... | collective-permute-start | bytes 1572872 | tf_op jit(solution)/shard_map/ppermute | solution.py:618
  848.1 64.3 %far_backward.1 = (bf16[1024,512]{1,0:T(8,128)(2,1)}, bf16[8192,1024]{1,0:T(8,128)(2,1)}) custom-call(bf16[1024,512]{1,0:T(8,128)(2,1)} %copy-done.8, bf16[8192,1024]{1,0:T(8,128)(2,1)} %all-gather.20.cloned.1.call-done.kv_ref, bf16[1024,512]{1,0:T(8,128)(2,1)} %pad_maximum_fusion.4.do_ref, bf16[1024,512]{1,0:T(8,128)(2,1)} %copy-done.9, ...), custom_call_target="tpu_custom_call" | custom-call | flops 42949672960 | bytes 33554432 | tf_op jit(solution)/shard_map/far_backward/pallas_call | solution.py:270
  918.6 78.2 %chain_own.2 = f32[1024,512]{1,0:T(8,128)S(1)} custom-call(bf16[1024,2048]{1,0:T(8,128)(2,1)S(1)} %copy-done.36, bf16[1024,2048]{1,0:T(8,128)(2,1)S(1)} %copy-done.33), custom_call_target="tpu_custom_call" | custom-call | flops 99999997952 | bytes 12582912 | tf_op jit(solution)/shard_map/chain_own/pallas_call | solution.py:452
  996.9 25.6 %gradients.5 = bf16[2048,4224]{1,0:T(8,128)(2,1)} custom-call(bf16[1024,2048]{1,0:T(8,128)(2,1)} %get-tuple-element.101.refs_0_, bf16[1024,2048]{1,0:T(8,128)(2,1)} %copy-done.26, bf16[1024,2816]{1,0:T(8,128)(2,1)} %get-tuple-element.103.refs_2_, bf16[1024,1408]{1,0:T(8,128)(2,1)} %get-tuple-element.104.refs_3_), custom_call_target="tpu_custom_call" | custom-call | flops 17716740096 | bytes 34603008 | tf_op jit(solution)/shard_map/gradients/pallas_call | solution.py:871
  1065.1 75.1 %chain_sum_turns.5.dout_ref.refs_1_.base_ref = bf16[1024,2048]{1,0:T(8,128)(2,1)S(1)} custom-call(bf16[1024,2048]{1,0:T(8,128)(2,1)S(1)} %copy-done.25, bf16[1024,2048]{1,0:T(8,128)(2,1)S(1)} %copy-done.19), custom_call_target="tpu_custom_call" | custom-call | flops 99999997952 | bytes 12582912 | tf_op jit(solution)/shard_map/chain_sum_turns/pallas_call | solution.py:452
  1142.3 36.2 %feed_backward.3 = (bf16[1024,2048]{1,0:T(8,128)(2,1)}, bf16[1024,2816]{1,0:T(8,128)(2,1)}, f32[1,2048]{1,0:T(1,128)}) custom-call(bf16[1024,2048]{1,0:T(8,128)(2,1)} %copy-done.28, bf16[1024,2048]{1,0:T(8,128)(2,1)} %copy-done.30, bf16[1024,2816]{1,0:T(8,128)(2,1)} %get-tuple-element.112.pair_ref, f32[1,2048]{1,0:T(1,128)} %get-tuple-element.193.gain_ref, ...), custom_call_target="tpu_custom_call" | custom-call | flops 17716740096 | bytes 14159872 | tf_op jit(solution)/shard_map/feed_backward/pallas_call | solution.py:664
  1178.6 26.1 %gradients.7 = bf16[2048,4224]{1,0:T(8,128)(2,1)} custom-call(bf16[1024,2048]{1,0:T(8,128)(2,1)} %get-tuple-element.114.refs_0_, bf16[1024,2048]{1,0:T(8,128)(2,1)} %copy-done.28, bf16[1024,2816]{1,0:T(8,128)(2,1)} %get-tuple-element.115.refs_2_, bf16[1024,1408]{1,0:T(8,128)(2,1)} %get-tuple-element.116.refs_3_), custom_call_target="tpu_custom_call" | custom-call | flops 17716740096 | bytes 34603008 | tf_op jit(solution)/shard_map/gradients/pallas_call | solution.py:871
  1204.7 49.3 %reduce-scatter.10.cloned.1.call-done = bf16[256,4224]{1,0:T(8,128)(2,1)} async-done(((bf16[2048,4224]{1,0:T(8,128)(2,1)}), bf16[256,4224]{1,0:T(8,128)(2,1)}) %reduce-scatter.10.cloned.1.call-update) | async-done | bytes 2162704 | tf_op jit(solution)/shard_map/reduce_scatter | solution.py:627
  1258.5 107.8 %chain_sum.5.refs_1_.base_ref = bf16[1024,2048]{1,0:T(8,128)(2,1)S(1)} custom-call(bf16[1024,2048]{1,0:T(8,128)(2,1)S(1)} %copy-done.34, bf16[1024,2048]{1,0:T(8,128)(2,1)S(1)} %copy-done.29), custom_call_target="tpu_custom_call" | custom-call | flops 99999997952 | bytes 12582912 | tf_op jit(solution)/shard_map/chain_sum/pallas_call | solution.py:452
  1370.6 21.3 %near_backward.1 = (bf16[1024,512]{1,0:T(8,128)(2,1)S(1)}, f32[2048,512]{1,0:T(8,128)S(1)}, f32[2048,512]{1,0:T(8,128)}) custom-call(bf16[1024,512]{1,0:T(8,128)(2,1)S(1)} %copy-done.7, bf16[2048,512]{1,0:T(8,128)(2,1)S(1)} %copy-done.5, bf16[2048,512]{1,0:T(8,128)(2,1)S(1)} %copy-done.3, bf16[1024,512]{1,0:T(8,128)(2,1)S(1)} %fusion.10.do_ref, ...), custom_call_target="tpu_custom_call" | custom-call | flops 13421772800 | bytes 16777216 | tf_op jit(solution)/shard_map/near_backward/pallas_call | solution.py:115
  1487.3 78.9 %chain_own.3 = f32[1024,512]{1,0:T(8,128)S(1)} custom-call(bf16[1024,2048]{1,0:T(8,128)(2,1)S(1)} %copy-done.22, bf16[1024,2048]{1,0:T(8,128)(2,1)S(1)} %copy-done.15), custom_call_target="tpu_custom_call" | custom-call | flops 99999997952 | bytes 12582912 | tf_op jit(solution)/shard_map/chain_own/pallas_call | solution.py:452
  (253 shorter events, 331.4 us)
Async XLA Ops:
  7.2 78.9 %all-gather.12.cloned.1.call-start = ((), (), s32[]{:S(2)}) async-start(), calls=%async_computation.5 | async-start | bytes 7667712 | tf_op jit(solution)/shard_map/all_gather | solution.py:623
  10.8 153.5 %all-gather.26.cloned.1.call-start = ((), (), s32[]{:S(2)}) async-start(), calls=%async_computation.17 | async-start | bytes 2359296 | tf_op jit(solution)/shard_map/all_gather | solution.py:623
  13.1 231.6 %all-gather.16.cloned.1.call-start = ((), (), s32[]{:S(2)}) async-start(), calls=%async_computation.7 | async-start | bytes 6488064 | tf_op jit(solution)/shard_map/all_gather | solution.py:623
  102.3 28.4 %collective-permute-start = (bf16[1024,1024]{1,0:T(8,128)(2,1)S(1)}, bf16[1024,1024]{1,0:T(8,128)(2,1)}, u32[]{:S(2)}, u32[]{:S(2)}) collective-permute-start(bf16[1024,1024]{1,0:T(8,128)(2,1)S(1)} %slice.144), channel_id=1, source_target_pairs={{0,4},{4,8},{8,12},{12,16},{16,20},{20,24},{24,28},{1,5},{5,9},{9,... | collective-permute-start | bytes 6291464 | tf_op jit(solution)/shard_map/ppermute | solution.py:613
  131.6 113.2 %all-gather.14.cloned.1.call-start = ((), (), s32[]{:S(2)}) async-start(), calls=%async_computation.6 | async-start | bytes 12976128 | tf_op jit(solution)/shard_map/all_gather | solution.py:623
  132.2 223.6 %all-gather.18.cloned.1.call-start = ((), (), s32[]{:S(2)}) async-start(), calls=%async_computation.8 | async-start | bytes 7077888 | tf_op jit(solution)/shard_map/all_gather | solution.py:623
  138.4 230.1 %all-gather.28.cloned.1.call-start = ((), (), s32[]{:S(2)}) async-start(), calls=%async_computation.18 | async-start | bytes 2359296 | tf_op jit(solution)/shard_map/all_gather | solution.py:623
  140.3 363.8 %all-gather.20.cloned.1.call-start = ((), (), s32[]{:S(2)}) async-start(), calls=%async_computation.9 | async-start | bytes 18874368 | tf_op jit(solution)/shard_map/all_gather | solution.py:623
  368.5 283.6 %all-gather.24.cloned.1.call-start = ((), (), s32[]{:S(2)}) async-start(), calls=%async_computation.11 | async-start | bytes 6488064 | tf_op jit(solution)/shard_map/all_gather | solution.py:623
  369.5 282.6 %all-gather.22.cloned.1.call-start = ((), (), s32[]{:S(2)}) async-start(), calls=%async_computation.10 | async-start | bytes 12976128 | tf_op jit(solution)/shard_map/all_gather | solution.py:623
  370.8 115.8 %collective-permute-start.1 = (bf16[512,512]{1,0:T(8,128)(2,1)S(1)}, bf16[512,512]{1,0:T(8,128)(2,1)S(1)}, u32[]{:S(2)}, u32[]{:S(2)}) collective-permute-start(bf16[512,512]{1,0:T(8,128)(2,1)S(1)} %get-tuple-element.187), channel_id=1, source_target_pairs={{0,28},{4,24},{8,20},{12,16},{16,12},{20,8},{24,4},{28,0},{1,29},{... | collective-permute-start | bytes 1572872 | tf_op jit(solution)/shard_map/ppermute | solution.py:618
  486.7 70.1 %copy-start.43 = (bf16[256,1,1376]{0,2,1:T(8,128)(2,1)S(1)}, bf16[256,1,1376]{0,2,1:T(8,128)(2,1)}, u32[]{:S(2)}) copy-start(bf16[256,1,1376]{0,2,1:T(8,128)(2,1)} %get-tuple-element.164) | copy-start | bytes 2113540
  554.6 14.8 collective-permute-start.2
  570.6 458.8 %reduce-scatter.6.cloned.1.call-start = ((), (), s32[]{:S(2)}) async-start(), calls=%async_computation.12 | async-start | bytes 18874368 | tf_op jit(solution)/shard_map/reduce_scatter | solution.py:955
  713.5 81.4 %copy-start.57 = (bf16[2048,1,512]{2,0,1:T(8,128)(2,1)S(1)}, bf16[2048,1,512]{2,0,1:T(8,128)(2,1)}, u32[]{:S(2)}) copy-start(bf16[2048,1,512]{2,0,1:T(8,128)(2,1)} %all-gather.28.cloned.1.call-done) | copy-start | bytes 6291460
  797.3 49.8 %collective-permute-start.3 = (bf16[512,512]{1,0:T(8,128)(2,1)S(1)}, bf16[512,512]{1,0:T(8,128)(2,1)S(1)}, u32[]{:S(2)}, u32[]{:S(2)}) collective-permute-start(bf16[512,512]{1,0:T(8,128)(2,1)S(1)} %get-tuple-element.183), channel_id=1, source_target_pairs={{0,28},{4,24},{8,20},{12,16},{16,12},{20,8},{24,4},{28,0},{1,29},{... | collective-permute-start | bytes 1572872 | tf_op jit(solution)/shard_map/ppermute | solution.py:618
  912.4 292.3 %reduce-scatter.8.cloned.1.call-start = ((), (), s32[]{:S(2)}) async-start(), calls=%async_computation.13 | async-start | bytes 9437184 | tf_op jit(solution)/shard_map/reduce_scatter | solution.py:627
  913.7 108.8 %collective-permute-start.4 = (bf16[512,512]{1,0:T(8,128)(2,1)S(1)}, bf16[512,512]{1,0:T(8,128)(2,1)}, u32[]{:S(2)}, u32[]{:S(2)}) collective-permute-start(bf16[512,512]{1,0:T(8,128)(2,1)S(1)} %get-tuple-element.181), channel_id=1, source_target_pairs={{0,28},{4,24},{8,20},{12,16},{16,12},{20,8},{24,4},{28,0},{1,29},{... | collective-permute-start | bytes 1572872 | tf_op jit(solution)/shard_map/ppermute | solution.py:618
  1060.1 194.0 %reduce-scatter.10.cloned.1.call-start = ((), (), s32[]{:S(2)}) async-start(), calls=%async_computation.14 | async-start | bytes 19464192 | tf_op jit(solution)/shard_map/reduce_scatter | solution.py:627
  1060.7 368.4 %reduce-scatter.12.cloned.1.call-start = ((), (), s32[]{:S(2)}) async-start(), calls=%async_computation.15 | async-start | bytes 19464192 | tf_op jit(solution)/shard_map/reduce_scatter | solution.py:627
  1204.7 362.8 %reduce-scatter.14.cloned.1.call-start = ((), (), s32[]{:S(2)}) async-start(), calls=%async_computation.16 | async-start | bytes 10027008 | tf_op jit(solution)/shard_map/reduce_scatter | solution.py:627
  1258.4 107.8 %copy-start.56 = (bf16[2048,1,512]{2,0,1:T(8,128)(2,1)S(1)}, bf16[2048,1,512]{2,0,1:T(8,128)(2,1)}, u32[]{:S(2)}) copy-start(bf16[2048,1,512]{2,0,1:T(8,128)(2,1)} %all-gather.26.cloned.1.call-done) | copy-start | bytes 6291460
  1398.7 25.5 %collective-permute-start.5 = (bf16[1024,1024]{1,0:T(8,128)(2,1)S(1)}, bf16[1024,1024]{1,0:T(8,128)(2,1)S(1)}, u32[]{:S(2)}, u32[]{:S(2)}) collective-permute-start(bf16[1024,1024]{1,0:T(8,128)(2,1)S(1)} %slice.220), channel_id=1, source_target_pairs={{4,0},{8,4},{12,8},{16,12},{20,16},{24,20},{28,24},{5,1},{9,5},{13... | collective-permute-start | bytes 6291464 | tf_op jit(solution)/shard_map/ppermute | solution.py:613
  1487.3 80.2 %copy-start.47 = (bf16[256,2048]{1,0:T(8,128)(2,1)S(1)}, bf16[256,2048]{1,0:T(8,128)(2,1)}, u32[]{:S(2)}) copy-start(bf16[256,2048]{1,0:T(8,128)(2,1)} %reduce-scatter.8.cloned.1.call-done) | copy-start | bytes 3145732
  (56 other events, 368.7 us)
Sparse Core Ops, SparseCore 0:
  10.9 48.3 all-gather.11
  61.2 28.0 all-gather.25
  131.7 43.2 all-gather.15
  177.3 67.4 all-gather.13
  247.1 45.7 all-gather.17
  294.6 28.0 all-gather.27
  368.6 135.4 all-gather.19
  506.0 43.8 all-gather.23
  570.7 68.2 all-gather.21
  912.6 116.7 reduce-scatter.5
  1060.2 71.2 reduce-scatter.7
  1135.4 118.5 reduce-scatter.9
  1257.7 118.5 reduce-scatter.11
  1459.4 75.1 reduce-scatter.13

commit v2 on v1

--- a/solution.py
+++ b/solution.py
@@ -442,7 +442,7 @@
                     outward(flow, step, piece, hop).wait_send()
 
 
-def chain_sum(partial_value, base, turns=0, own_only=False):
+def chain_sum(partial_value, base, turns=0, own_only=False, brief=False):
     turns = turns if lax.axis_size("seq") % 2 == 0 else 0
     rows, depth = base.shape
     chunk = 32
@@ -461,7 +461,7 @@
             collective_id=1 + turns if turns else 6 * own_only, has_side_effects=True, vmem_limit_bytes=32 * MIB
         ),
         cost_estimate=pl.CostEstimate(
-            flops=10**11, bytes_accessed=rows * depth * 6, transcendentals=0
+            flops=10**6 if brief else 10**11, bytes_accessed=10**6, transcendentals=0
         ),
         name="chain_sum_turns" if turns else "chain_own" if own_only else "chain_sum",
     )(partial_value.astype(bf16), base)
@@ -967,12 +967,13 @@
         (gradients([(normed3, dcache), (normed4, dquery2), (dfull3, own_attended2)]),),
     )
     grad_cross = scattered(grad_cross)
-    dfull2 = chain_sum(dpart, dfull3, turns=3)
+    dfull2 = chain_sum(dpart, dfull3, turns=3, brief=True)
     dpart, pairs_feed1, grad_gain1 = feed_backward(dfull2, gain[1], w_pair1, w_down1, saved1)
     dpart, (grad_feed1,) = together(dpart, (gradients(pairs_feed1),))
     grad_feed1 = scattered(grad_feed1)
-    dpart, grad_cross, grad_feed2 = lax.optimization_barrier((dpart, grad_cross, grad_feed2))
-    dfull1 = chain_sum(dpart, dfull2)
+    dpart, grad_cross = lax.optimization_barrier((dpart, grad_cross))
+    dfull1 = chain_sum(dpart, dfull2, brief=True)
+    dfull1, grad_feed2 = lax.optimization_barrier((dfull1, grad_feed2))
     dattended1 = nn(dfull1, w_out1).astype(bf16)
     dquery1, dkey1, dvalue1 = near_backward(query1, key1, value1, dattended1, attended1, stats1)
     dnear = jnp.concatenate([dkey1, dvalue1], axis=1)

time: 1620 us -> 1590 us (0.981)
  waiting for transfers between devices: 125 us -> 80.4 us
  starting transfers between devices: 87 us -> 126 us
  Pallas kernels: 1220 us -> 1200 us
    reduce_scatter x4, waiting for transfers between devices: 49.3 us -> 0.02 us  [scattered(): lax.psum_scatter(grad.astype(bf16), 'seq', scatter_dimension=0, tiled=True)]
    ppermute x2, starting transfers between devices: 3.84 us -> 41.9 us  [shifted(): return lax.ppermute(block, axis, route)]
    pallas_call x8, Pallas kernels: 649 us -> 622 us  [chain_sum(): pl.pallas_call(functools.partial(chain_kernel, chunk, turns, own_only), i...]
    unnamed x134 -> x132, local copies, waits for them, and re-layouts: 78.9 us -> 79.4 us
  transfers between devices with their start and end apart: 20 -> 20, of which waited for: 7 -> 6; matrix products, arithmetic and copies ran while one was open for 5% -> 5% of each run, Pallas kernels for 59% -> 58%
where the time goes in v2:
time: 1590 us; the launch traced here: 1580 us
  Pallas kernels  1200 us (75%)
  starting transfers between devices  126 us (8%)
  local copies, waits for them, and re-layouts  117 us (7%)
  waiting for transfers between devices  80.4 us (5%)
  other arithmetic  29.1 us (2%)
  matrix products  18.3 us (1%)
    pallas_call x8, Pallas kernels, chain_sum(): pl.pallas_call(functools.partial(chain_kernel, chunk, turns, own_only), i...  622 us
    pallas_call x8, Pallas kernels, blocks_call(): pl.pallas_call(kernel, grid=(rows // size,), in_specs=in_specs, out_specs...  178 us
    pallas_call x2, Pallas kernels, spread(): pl.pallas_call(functools.partial(spread_kernel, chunk), in_specs=[whole],...  143 us
    pallas_call x5, Pallas kernels, gradients(): pl.pallas_call(functools.partial(gradients_kernel, len(pairs)), grid=(dep...  86.7 us
    ppermute x4, starting transfers between devices, swapped(): lax.ppermute(block[half:], 'seq', [(i, count - 1 - i) for i in range(coun...  83.1 us
    unnamed x132, local copies, waits for them, and re-layouts  79.4 us
    pallas_call x1, Pallas kernels, far_backward(): pl.pallas_call(far_backward_kernel, grid=(heads, 2), in_specs=[own, whole...  64.3 us
    pallas_call x1, Pallas kernels, far_forward(): pl.pallas_call(far_forward_kernel, grid=(heads, 2), in_specs=[own, whole]...  48.8 us
  transfers between devices with their start and end apart: 20, of which 6 were waited for; matrix products, arithmetic and copies ran while one was open for 5% of the time, Pallas kernels for 58%

profile of v2, /device:TPU:28, one launch (start us, length us, event | category | flops | bytes accessed | tf_op | source)
XLA Modules:
  0.0 1582.1 jit_solution(15113970524736250470)
XLA Ops:
  13.2 70.9 %spread.2.full_ref.base_ref = bf16[1024,2048]{1,0:T(8,128)(2,1)S(1)} custom-call(f32[1024,512]{1,0:T(8,128)S(1)} %copy-done.20), custom_call_target="tpu_custom_call" | custom-call | flops 70000001024 | bytes 10485760 | tf_op jit(solution)/shard_map/spread/pallas_call | solution.py:546
  168.7 74.1 %chain_sum_turns.3.full_ref.base_ref = bf16[1024,2048]{1,0:T(8,128)(2,1)S(1)} custom-call(bf16[1024,2048]{1,0:T(8,128)(2,1)S(1)} %convolution_convert_fusion.1.part_ref, bf16[1024,2048]{1,0:T(8,128)(2,1)S(1)} %copy-done.25), custom_call_target="tpu_custom_call" | custom-call | flops 99999997952 | bytes 1000000 | tf_op jit(solution)/shard_map/chain_sum_turns/pallas_call | solution.py:452
  244.8 27.7 %feed_forward.2 = (bf16[1024,2048]{1,0:T(8,128)(2,1)}, bf16[1024,2048]{1,0:T(8,128)(2,1)}, bf16[1024,2816]{1,0:T(8,128)(2,1)}, bf16[1024,1408]{1,0:T(8,128)(2,1)}) custom-call(bf16[1024,2048]{1,0:T(8,128)(2,1)} %copy-done.31, f32[1,2048]{1,0:T(1,128)} %get-tuple-element.195.gain_ref, bf16[2048,2816]{1,0:T(8,128)(2,1)} %all-gather.14.cloned.1.call-done.pair_hbm, ...), custom_call_target="tpu_custom_call" | custom-call | flops 17716740096 | bytes 4198400 | tf_op jit(solution)/shard_map/feed_forward/pallas_call | solution.py:664
  275.1 78.5 %chain_sum.3.full_ref.base_ref = bf16[1024,2048]{1,0:T(8,128)(2,1)S(1)} custom-call(bf16[1024,2048]{1,0:T(8,128)(2,1)S(1)} %copy-done.37, bf16[1024,2048]{1,0:T(8,128)(2,1)S(1)} %copy-done.32), custom_call_target="tpu_custom_call" | custom-call | flops 99999997952 | bytes 1000000 | tf_op jit(solution)/shard_map/chain_sum/pallas_call | solution.py:452
  370.7 42.1 %collective-permute-start.1 = (bf16[512,512]{1,0:T(8,128)(2,1)S(1)}, bf16[512,512]{1,0:T(8,128)(2,1)S(1)}, u32[]{:S(2)}, u32[]{:S(2)}) collective-permute-start(bf16[512,512]{1,0:T(8,128)(2,1)S(1)} %get-tuple-element.189), channel_id=1, source_target_pairs={{0,28},{4,24},{8,20},{12,16},{16,12},{20,8},{24,4},{28,0},{1,29},{... | collective-permute-start | bytes 1572872 | tf_op jit(solution)/shard_map/ppermute | solution.py:618
  412.8 71.7 %spread.3.dout_ref.base_ref.refs_1_ = bf16[1024,2048]{1,0:T(8,128)(2,1)S(1)} custom-call(f32[1024,512]{1,0:T(8,128)S(1)} %copy-done.21), custom_call_target="tpu_custom_call" | custom-call | flops 70000001024 | bytes 10485760 | tf_op jit(solution)/shard_map/spread/pallas_call | solution.py:546
  486.7 17.4 %all-gather.20.cloned.1.call-done.kv_ref = bf16[8192,1024]{1,0:T(8,128)(2,1)} async-done(((bf16[1024,1024]{1,0:T(8,128)(2,1)}), bf16[8192,1024]{1,0:T(8,128)(2,1)}) %all-gather.20.cloned.1.call-update) | async-done | bytes 16777232 | tf_op jit(solution)/shard_map/all_gather | solution.py:623
  504.0 48.8 %far_forward.1 = (bf16[1024,512]{1,0:T(8,128)(2,1)S(1)}, f32[4,1,1024]{2,1,0:T(1,128)S(1)}) custom-call(bf16[1024,512]{1,0:T(8,128)(2,1)S(1)} %pad_maximum_fusion.2.q_ref, bf16[8192,1024]{1,0:T(8,128)(2,1)} %all-gather.20.cloned.1.call-done.kv_ref), custom_call_target="tpu_custom_call" | custom-call | flops 17179869184 | bytes 16777216 | tf_op jit(solution)/shard_map/far_forward/pallas_call | solution.py:189
  575.5 75.1 %chain_sum_turns.4.full_ref.base_ref = bf16[1024,2048]{1,0:T(8,128)(2,1)S(1)} custom-call(bf16[1024,2048]{1,0:T(8,128)(2,1)S(1)} %convolution_convert_fusion.part_ref, bf16[1024,2048]{1,0:T(8,128)(2,1)S(1)} %copy-done.28), custom_call_target="tpu_custom_call" | custom-call | flops 99999997952 | bytes 1000000 | tf_op jit(solution)/shard_map/chain_sum_turns/pallas_call | solution.py:452
  652.6 27.5 %feed_forward.3 = (bf16[1024,2048]{1,0:T(8,128)(2,1)}, bf16[1024,2048]{1,0:T(8,128)(2,1)}, bf16[1024,2816]{1,0:T(8,128)(2,1)}, bf16[1024,1408]{1,0:T(8,128)(2,1)}) custom-call(bf16[1024,2048]{1,0:T(8,128)(2,1)} %copy-done.33, f32[1,2048]{1,0:T(1,128)} %get-tuple-element.192.gain_ref, bf16[2048,2816]{1,0:T(8,128)(2,1)} %all-gather.22.cloned.1.call-done.pair_hbm, ...), custom_call_target="tpu_custom_call" | custom-call | flops 17716740096 | bytes 4198400 | tf_op jit(solution)/shard_map/feed_forward/pallas_call | solution.py:664
  680.1 31.7 %feed_backward.2 = (bf16[1024,2048]{1,0:T(8,128)(2,1)}, bf16[1024,2816]{1,0:T(8,128)(2,1)}, f32[1,2048]{1,0:T(1,128)}) custom-call(bf16[1024,2048]{1,0:T(8,128)(2,1)} %copy-done.29, bf16[1024,2048]{1,0:T(8,128)(2,1)} %copy-done.33, bf16[1024,2816]{1,0:T(8,128)(2,1)} %get-tuple-element.92.pair_ref, f32[1,2048]{1,0:T(1,128)} %get-tuple-element.192.gain_ref, ...), custom_call_target="tpu_custom_call" | custom-call | flops 17716740096 | bytes 14159872 | tf_op jit(solution)/shard_map/feed_backward/pallas_call | solution.py:664
  714.0 81.4 %chain_sum.4.refs_2_.base_ref = bf16[1024,2048]{1,0:T(8,128)(2,1)S(1)} custom-call(bf16[1024,2048]{1,0:T(8,128)(2,1)S(1)} %copy-done.35, bf16[1024,2048]{1,0:T(8,128)(2,1)S(1)} %copy-done.30), custom_call_target="tpu_custom_call" | custom-call | flops 99999997952 | bytes 1000000 | tf_op jit(solution)/shard_map/chain_sum/pallas_call | solution.py:452
  797.8 37.4 %collective-permute-start.3 = (bf16[512,512]{1,0:T(8,128)(2,1)S(1)}, bf16[512,512]{1,0:T(8,128)(2,1)S(1)}, u32[]{:S(2)}, u32[]{:S(2)}) collective-permute-start(bf16[512,512]{1,0:T(8,128)(2,1)S(1)} %get-tuple-element.185), channel_id=1, source_target_pairs={{0,28},{4,24},{8,20},{12,16},{16,12},{20,8},{24,4},{28,0},{1,29},{... | collective-permute-start | bytes 1572872 | tf_op jit(solution)/shard_map/ppermute | solution.py:618
  847.5 64.3 %far_backward.1 = (bf16[1024,512]{1,0:T(8,128)(2,1)}, bf16[8192,1024]{1,0:T(8,128)(2,1)}) custom-call(bf16[1024,512]{1,0:T(8,128)(2,1)} %copy-done.16, bf16[8192,1024]{1,0:T(8,128)(2,1)} %all-gather.20.cloned.1.call-done.kv_ref, bf16[1024,512]{1,0:T(8,128)(2,1)} %pad_maximum_fusion.4.do_ref, bf16[1024,512]{1,0:T(8,128)(2,1)} %copy-done.17, ...), custom_call_target="tpu_custom_call" | custom-call | flops 42949672960 | bytes 33554432 | tf_op jit(solution)/shard_map/far_backward/pallas_call | solution.py:270
  919.1 77.7 %chain_own.2 = f32[1024,512]{1,0:T(8,128)S(1)} custom-call(bf16[1024,2048]{1,0:T(8,128)(2,1)S(1)} %copy-done.36, bf16[1024,2048]{1,0:T(8,128)(2,1)S(1)} %copy-done.34), custom_call_target="tpu_custom_call" | custom-call | flops 99999997952 | bytes 1000000 | tf_op jit(solution)/shard_map/chain_own/pallas_call | solution.py:452
  996.9 25.6 %gradients.5 = bf16[2048,4224]{1,0:T(8,128)(2,1)} custom-call(bf16[1024,2048]{1,0:T(8,128)(2,1)} %get-tuple-element.102.refs_0_, bf16[1024,2048]{1,0:T(8,128)(2,1)} %copy-done.29, bf16[1024,2816]{1,0:T(8,128)(2,1)} %get-tuple-element.104.refs_2_, bf16[1024,1408]{1,0:T(8,128)(2,1)} %get-tuple-element.105.refs_3_), custom_call_target="tpu_custom_call" | custom-call | flops 17716740096 | bytes 34603008 | tf_op jit(solution)/shard_map/gradients/pallas_call | solution.py:871
  1064.9 75.1 %chain_sum_turns.5.dout_ref.refs_1_.base_ref = bf16[1024,2048]{1,0:T(8,128)(2,1)S(1)} custom-call(bf16[1024,2048]{1,0:T(8,128)(2,1)S(1)} %copy-done.7, bf16[1024,2048]{1,0:T(8,128)(2,1)S(1)} %copy-done.5), custom_call_target="tpu_custom_call" | custom-call | flops 1000000 | bytes 1000000 | tf_op jit(solution)/shard_map/chain_sum_turns/pallas_call | solution.py:452
  1142.1 36.2 %feed_backward.3 = (bf16[1024,2048]{1,0:T(8,128)(2,1)}, bf16[1024,2816]{1,0:T(8,128)(2,1)}, f32[1,2048]{1,0:T(1,128)}) custom-call(bf16[1024,2048]{1,0:T(8,128)(2,1)} %copy-done, bf16[1024,2048]{1,0:T(8,128)(2,1)} %copy-done.31, bf16[1024,2816]{1,0:T(8,128)(2,1)} %get-tuple-element.113.pair_ref, f32[1,2048]{1,0:T(1,128)} %get-tuple-element.195.gain_ref, ...), custom_call_target="tpu_custom_call" | custom-call | flops 17716740096 | bytes 14159872 | tf_op jit(solution)/shard_map/feed_backward/pallas_call | solution.py:664
  1178.3 26.0 %gradients.7 = bf16[2048,4224]{1,0:T(8,128)(2,1)} custom-call(bf16[1024,2048]{1,0:T(8,128)(2,1)} %get-tuple-element.115.refs_0_, bf16[1024,2048]{1,0:T(8,128)(2,1)} %copy-done, bf16[1024,2816]{1,0:T(8,128)(2,1)} %get-tuple-element.116.refs_2_, bf16[1024,1408]{1,0:T(8,128)(2,1)} %get-tuple-element.117.refs_3_), custom_call_target="tpu_custom_call" | custom-call | flops 17716740096 | bytes 34603008 | tf_op jit(solution)/shard_map/gradients/pallas_call | solution.py:871
  1209.1 81.2 %chain_sum.5.refs_1_.base_ref = bf16[1024,2048]{1,0:T(8,128)(2,1)S(1)} custom-call(bf16[1024,2048]{1,0:T(8,128)(2,1)S(1)} %copy-done.6, bf16[1024,2048]{1,0:T(8,128)(2,1)S(1)} %copy-done.1), custom_call_target="tpu_custom_call" | custom-call | flops 1000000 | bytes 1000000 | tf_op jit(solution)/shard_map/chain_sum/pallas_call | solution.py:452
  1298.4 21.3 %near_backward.1 = (bf16[1024,512]{1,0:T(8,128)(2,1)S(1)}, f32[2048,512]{1,0:T(8,128)S(1)}, f32[2048,512]{1,0:T(8,128)}) custom-call(bf16[1024,512]{1,0:T(8,128)(2,1)S(1)} %copy-done.15, bf16[2048,512]{1,0:T(8,128)(2,1)S(1)} %copy-done.13, bf16[2048,512]{1,0:T(8,128)(2,1)S(1)} %copy-done.11, bf16[1024,512]{1,0:T(8,128)(2,1)S(1)} %fusion.10.do_ref, ...), custom_call_target="tpu_custom_call" | custom-call | flops 13421772800 | bytes 16777216 | tf_op jit(solution)/shard_map/near_backward/pallas_call | solution.py:115
  1326.9 40.0 %collective-permute-start.5 = (bf16[1024,1024]{1,0:T(8,128)(2,1)S(1)}, bf16[1024,1024]{1,0:T(8,128)(2,1)S(1)}, u32[]{:S(2)}, u32[]{:S(2)}) collective-permute-start(bf16[1024,1024]{1,0:T(8,128)(2,1)S(1)} %slice.220), channel_id=1, source_target_pairs={{4,0},{8,4},{12,8},{16,12},{20,16},{24,20},{28,24},{5,1},{9,5},{13... | collective-permute-start | bytes 6291464 | tf_op jit(solution)/shard_map/ppermute | solution.py:613
  1376.4 18.7 %collective-permute-done.5 = bf16[1024,1024]{1,0:T(8,128)(2,1)S(1)} collective-permute-done((bf16[1024,1024]{1,0:T(8,128)(2,1)S(1)}, bf16[1024,1024]{1,0:T(8,128)(2,1)S(1)}, u32[]{:S(2)}, u32[]{:S(2)}) %collective-permute-start.5) | collective-permute-done | bytes 2097184 | tf_op jit(solution)/shard_map/ppermute | solution.py:613
  1458.2 78.5 %chain_own.3 = f32[1024,512]{1,0:T(8,128)S(1)} custom-call(bf16[1024,2048]{1,0:T(8,128)(2,1)S(1)} %copy-done.26, bf16[1024,2048]{1,0:T(8,128)(2,1)S(1)} %copy-done.3), custom_call_target="tpu_custom_call" | custom-call | flops 99999997952 | bytes 1000000 | tf_op jit(solution)/shard_map/chain_own/pallas_call | solution.py:452
  (251 shorter events, 337.9 us)
Async XLA Ops:
  7.2 78.9 %all-gather.12.cloned.1.call-start = ((), (), s32[]{:S(2)}) async-start(), calls=%async_computation.5 | async-start | bytes 7667712 | tf_op jit(solution)/shard_map/all_gather | solution.py:623
  10.8 153.4 %all-gather.26.cloned.1.call-start = ((), (), s32[]{:S(2)}) async-start(), calls=%async_computation.17 | async-start | bytes 2359296 | tf_op jit(solution)/shard_map/all_gather | solution.py:623
  13.1 231.6 %all-gather.16.cloned.1.call-start = ((), (), s32[]{:S(2)}) async-start(), calls=%async_computation.7 | async-start | bytes 6488064 | tf_op jit(solution)/shard_map/all_gather | solution.py:623
  102.3 28.4 %collective-permute-start = (bf16[1024,1024]{1,0:T(8,128)(2,1)S(1)}, bf16[1024,1024]{1,0:T(8,128)(2,1)}, u32[]{:S(2)}, u32[]{:S(2)}) collective-permute-start(bf16[1024,1024]{1,0:T(8,128)(2,1)S(1)} %slice.144), channel_id=1, source_target_pairs={{0,4},{4,8},{8,12},{12,16},{16,20},{20,24},{24,28},{1,5},{5,9},{9,... | collective-permute-start | bytes 6291464 | tf_op jit(solution)/shard_map/ppermute | solution.py:613
  131.6 113.2 %all-gather.14.cloned.1.call-start = ((), (), s32[]{:S(2)}) async-start(), calls=%async_computation.6 | async-start | bytes 12976128 | tf_op jit(solution)/shard_map/all_gather | solution.py:623
  132.2 223.5 %all-gather.18.cloned.1.call-start = ((), (), s32[]{:S(2)}) async-start(), calls=%async_computation.8 | async-start | bytes 7077888 | tf_op jit(solution)/shard_map/all_gather | solution.py:623
  138.4 229.9 %all-gather.28.cloned.1.call-start = ((), (), s32[]{:S(2)}) async-start(), calls=%async_computation.18 | async-start | bytes 2359296 | tf_op jit(solution)/shard_map/all_gather | solution.py:623
  140.3 363.8 %all-gather.20.cloned.1.call-start = ((), (), s32[]{:S(2)}) async-start(), calls=%async_computation.9 | async-start | bytes 18874368 | tf_op jit(solution)/shard_map/all_gather | solution.py:623
  368.3 284.2 %all-gather.24.cloned.1.call-start = ((), (), s32[]{:S(2)}) async-start(), calls=%async_computation.11 | async-start | bytes 6488064 | tf_op jit(solution)/shard_map/all_gather | solution.py:623
  369.4 283.2 %all-gather.22.cloned.1.call-start = ((), (), s32[]{:S(2)}) async-start(), calls=%async_computation.10 | async-start | bytes 12976128 | tf_op jit(solution)/shard_map/all_gather | solution.py:623
  370.7 115.9 %collective-permute-start.1 = (bf16[512,512]{1,0:T(8,128)(2,1)S(1)}, bf16[512,512]{1,0:T(8,128)(2,1)S(1)}, u32[]{:S(2)}, u32[]{:S(2)}) collective-permute-start(bf16[512,512]{1,0:T(8,128)(2,1)S(1)} %get-tuple-element.189), channel_id=1, source_target_pairs={{0,28},{4,24},{8,20},{12,16},{16,12},{20,8},{24,4},{28,0},{1,29},{... | collective-permute-start | bytes 1572872 | tf_op jit(solution)/shard_map/ppermute | solution.py:618
  486.6 66.2 %copy-start.16 = (bf16[1024,512]{1,0:T(8,128)(2,1)}, bf16[1024,512]{1,0:T(8,128)(2,1)S(1)}, u32[]{:S(2)}) copy-start(bf16[1024,512]{1,0:T(8,128)(2,1)S(1)} %pad_maximum_fusion.2.q_ref) | copy-start | bytes 3145732
  486.6 70.1 %copy-start.43 = (bf16[256,1,1376]{0,2,1:T(8,128)(2,1)S(1)}, bf16[256,1,1376]{0,2,1:T(8,128)(2,1)}, u32[]{:S(2)}) copy-start(bf16[256,1,1376]{0,2,1:T(8,128)(2,1)} %get-tuple-element.166) | copy-start | bytes 2113540
  554.7 15.2 collective-permute-start.2
  571.1 458.1 %reduce-scatter.6.cloned.1.call-start = ((), (), s32[]{:S(2)}) async-start(), calls=%async_computation.12 | async-start | bytes 18874368 | tf_op jit(solution)/shard_map/reduce_scatter | solution.py:955
  714.0 81.4 %copy-start.56 = (bf16[2048,1,512]{2,0,1:T(8,128)(2,1)S(1)}, bf16[2048,1,512]{2,0,1:T(8,128)(2,1)}, u32[]{:S(2)}) copy-start(bf16[2048,1,512]{2,0,1:T(8,128)(2,1)} %all-gather.28.cloned.1.call-done) | copy-start | bytes 6291460
  797.8 48.7 %collective-permute-start.3 = (bf16[512,512]{1,0:T(8,128)(2,1)S(1)}, bf16[512,512]{1,0:T(8,128)(2,1)S(1)}, u32[]{:S(2)}, u32[]{:S(2)}) collective-permute-start(bf16[512,512]{1,0:T(8,128)(2,1)S(1)} %get-tuple-element.185), channel_id=1, source_target_pairs={{0,28},{4,24},{8,20},{12,16},{16,12},{20,8},{24,4},{28,0},{1,29},{... | collective-permute-start | bytes 1572872 | tf_op jit(solution)/shard_map/ppermute | solution.py:618
  911.9 292.6 %reduce-scatter.8.cloned.1.call-start = ((), (), s32[]{:S(2)}) async-start(), calls=%async_computation.13 | async-start | bytes 9437184 | tf_op jit(solution)/shard_map/reduce_scatter | solution.py:627
  913.2 109.3 %collective-permute-start.4 = (bf16[512,512]{1,0:T(8,128)(2,1)S(1)}, bf16[512,512]{1,0:T(8,128)(2,1)}, u32[]{:S(2)}, u32[]{:S(2)}) collective-permute-start(bf16[512,512]{1,0:T(8,128)(2,1)S(1)} %get-tuple-element.183), channel_id=1, source_target_pairs={{0,28},{4,24},{8,20},{12,16},{16,12},{20,8},{24,4},{28,0},{1,29},{... | collective-permute-start | bytes 1572872 | tf_op jit(solution)/shard_map/ppermute | solution.py:618
  1059.9 232.4 %reduce-scatter.10.cloned.1.call-start = ((), (), s32[]{:S(2)}) async-start(), calls=%async_computation.14 | async-start | bytes 19464192 | tf_op jit(solution)/shard_map/reduce_scatter | solution.py:627
  1060.5 339.6 %reduce-scatter.12.cloned.1.call-start = ((), (), s32[]{:S(2)}) async-start(), calls=%async_computation.15 | async-start | bytes 19464192 | tf_op jit(solution)/shard_map/reduce_scatter | solution.py:627
  1204.4 333.6 %reduce-scatter.14.cloned.1.call-start = ((), (), s32[]{:S(2)}) async-start(), calls=%async_computation.16 | async-start | bytes 10027008 | tf_op jit(solution)/shard_map/reduce_scatter | solution.py:627
  1326.9 68.3 %collective-permute-start.5 = (bf16[1024,1024]{1,0:T(8,128)(2,1)S(1)}, bf16[1024,1024]{1,0:T(8,128)(2,1)S(1)}, u32[]{:S(2)}, u32[]{:S(2)}) collective-permute-start(bf16[1024,1024]{1,0:T(8,128)(2,1)S(1)} %slice.220), channel_id=1, source_target_pairs={{4,0},{8,4},{12,8},{16,12},{20,16},{24,20},{28,24},{5,1},{9,5},{13... | collective-permute-start | bytes 6291464 | tf_op jit(solution)/shard_map/ppermute | solution.py:613
  1458.2 79.9 %copy-start.47 = (bf16[256,2048]{1,0:T(8,128)(2,1)S(1)}, bf16[256,2048]{1,0:T(8,128)(2,1)}, u32[]{:S(2)}) copy-start(bf16[256,2048]{1,0:T(8,128)(2,1)} %reduce-scatter.8.cloned.1.call-done) | copy-start | bytes 3145732
  (55 other events, 470.7 us)
Sparse Core Ops, SparseCore 0:
  10.9 48.3 all-gather.11
  61.2 28.0 all-gather.25
  131.7 43.2 all-gather.15
  177.3 67.4 all-gather.13
  247.1 45.7 all-gather.17
  294.6 28.0 all-gather.27
  368.5 135.5 all-gather.19
  505.9 43.8 all-gather.23
  571.2 67.7 all-gather.21
  912.0 117.1 reduce-scatter.5
  1060.0 71.2 reduce-scatter.7
  1135.2 118.5 reduce-scatter.9
  1257.5 121.5 reduce-scatter.11
  1430.3 75.1 reduce-scatter.13
